TPU v7x, 128 devices: a whole 4x4x4 slice. The times are simulated.
128 devices in a mesh: slab: 128 (over x, z, y, core).
Axes of the slice: x: 4, y: 4, z: 4, core: 2. Of those that a mesh axis runs over, the one named last changes fastest.
Arguments:
- positions: float32 [16384, 3, 128], P('slab'), may hold values from -1.2 to 1.2
- velocity: float32 [16384, 3, 128], P('slab'), may hold values from -6 to 6
- masses: float32 [16384, 128], P('slab'), may hold values from 0.5 to 2
- counts: int32 [16384], P('slab'), may hold values from 16 to 128, as said below
- pair_home: int32 [81920], P('slab'), may hold values from 0 to 127, as said below
- pair_far: int32 [81920], P('slab'), may hold values from 0 to 127, as said below
- pair_owner: int32 [81920], P('slab'), may hold values from 0 to 1, as said below
- cot_x: float32 [16384, 3, 128], P('slab'), may hold values from -6 to 6
- cot_v: float32 [16384, 3, 128], P('slab'), may hold values from -6 to 6
Outputs:
- new_x: float32 [16384, 3, 128], P('slab')
- new_v: float32 [16384, 3, 128], P('slab')
- grad_x: float32 [16384, 3, 128], P('slab')
- grad_v: float32 [16384, 3, 128], P('slab')
- grad_m: float32 [16384, 128], P('slab')
Inputs may be any that keep to these rules, and one draw needn't show every extreme that they name: counts[b] slots of block b hold particles, the rest are padding. `pair_home`: entries k * 640 to (k + 1) * 640 - 1 belong to slab k. Where pair_owner is 0, pair_far differs from pair_home. `pair_owner`: always 0 on the last slab.
All inputs are finite; a program needn't handle non-finite values.
Results may differ from a plain program's by a relative error of at most 0.00002.
Values sent between devices are 32-bit elements; how exact they have to be, the bound alone decides.
A program may use at most 64 MiB of HBM per device.

v0:
```python
import math

import jax
import jax.numpy as jnp
from jax import lax
from jax.sharding import PartitionSpec as P

DT = 0.1
VISCOSITY = 0.5
STIFFNESS = 0.5
RHO_FLOOR = 0.5
GRAVITY = 1.0
tile_batch = 32


def shifted(value, axis, by):
    devices = lax.axis_size(axis)
    pairs = [(i, i + by) for i in range(devices) if 0 <= i + by < devices]
    return lax.ppermute(value, axis, pairs)


def separation(a, b):
    offsets = a[:, 0:3, :, None] - b[:, 0:3, None, :]
    return (offsets, jnp.sum(offsets * offsets, axis=1))


def density_tile(a, b):
    offsets, square = separation(a, b)
    inside = jnp.maximum(1.0 - square, 0.0)
    kernel = inside * inside * inside
    to_a = jnp.sum(kernel * b[:, 6, None, :], axis=2) / a.shape[2]
    to_b = jnp.sum(kernel * a[:, 6, :, None], axis=1) / a.shape[2]
    return (to_a[:, None, :], to_b[:, None, :])


def force_tile(a, b):
    offsets, square = separation(a, b)
    inside = jnp.maximum(1.0 - square, 0.0)
    falloff = inside * inside
    kernel = falloff * inside
    pressure = 6.0 * (a[:, 7, :, None] + b[:, 7, None, :]) * falloff
    damping = VISCOSITY * kernel
    push_a = pressure * b[:, 6, None, :]
    push_b = pressure * a[:, 6, :, None]
    damp_a = damping * (b[:, 6] * b[:, 8])[:, None, :]
    damp_b = damping * (a[:, 6] * a[:, 8])[:, :, None]
    to_a = (
        jnp.sum(push_a[:, None] * offsets, axis=3)
        + jnp.sum(damp_a[:, None] * b[:, 3:6, None, :], axis=3)
        - a[:, 3:6] * jnp.sum(damp_a, axis=2)[:, None, :]
    )
    to_b = (
        -jnp.sum(push_b[:, None] * offsets, axis=2)
        + jnp.sum(damp_b[:, None] * a[:, 3:6, :, None], axis=2)
        - b[:, 3:6] * jnp.sum(damp_b, axis=1)[:, None, :]
    )
    return (to_a / a.shape[2], to_b / a.shape[2])


def eos_state(density):
    bounded = jnp.sqrt(density * density + RHO_FLOOR * RHO_FLOOR)
    return (STIFFNESS * (bounded * bounded * bounded - 1.0) / (bounded * bounded), 1.0 / bounded)


def grouped(first_idx, second_idx, first_w, second_w):
    group_size = math.gcd(first_idx.shape[0], tile_batch)
    return (
        first_idx.reshape(-1, group_size),
        second_idx.reshape(-1, group_size),
        first_w.reshape(-1, group_size),
        second_w.reshape(-1, group_size),
    )


def accumulate(tile_fn, table_in, first_idx, second_idx, first_w, second_w, height, channels):

    def accumulate_one_group(running, group):
        lead_idx, other_idx, lead_w, other_w = group
        to_a, to_b = tile_fn(table_in[lead_idx], table_in[other_idx])
        running = running.at[lead_idx].add(to_a * lead_w[:, None, None])
        running = running.at[other_idx].add(to_b * other_w[:, None, None])
        return (running, None)

    initial = jnp.zeros((height, channels, table_in.shape[2]), jnp.float32)
    return lax.scan(
        accumulate_one_group, initial, grouped(first_idx, second_idx, first_w, second_w)
    )[0]


def pull_back(tile_fn, table_in, first_idx, second_idx, first_w, second_w, cotangent):

    def pull_one_group(gradient, group):
        lead_idx, other_idx, lead_w, other_w = group
        _, backward = jax.vjp(tile_fn, table_in[lead_idx], table_in[other_idx])
        grad_a, grad_b = backward(
            (
                cotangent[lead_idx] * lead_w[:, None, None],
                cotangent[other_idx] * other_w[:, None, None],
            )
        )
        gradient = gradient.at[lead_idx].add(grad_a).at[other_idx].add(grad_b)
        return (gradient, None)

    initial = jnp.zeros(table_in.shape, jnp.float32)
    return lax.scan(pull_one_group, initial, grouped(first_idx, second_idx, first_w, second_w))[0]


def from_next(payload):
    return shifted(payload, "slab", -1)


def to_next(payload):
    return shifted(payload, "slab", 1)


def local(positions, velocity, masses, counts, pair_home, pair_far, pair_owner, cot_x, cot_v):
    blocks = positions.shape[0]
    pair_count = pair_home.shape[0]
    occupied = (lax.broadcasted_iota(jnp.int32, masses.shape, 1) < counts[:, None]).astype(
        jnp.float32
    )
    live_mass = masses * occupied
    particle_table = jnp.concatenate([positions, velocity, live_mass[:, None, :]], axis=1)
    own_block = jnp.arange(blocks, dtype=jnp.int32)
    next_table = from_next(particle_table)
    tables = jnp.concatenate([particle_table, next_table], axis=0)
    first_idx = jnp.concatenate([own_block, pair_home])
    second_idx = jnp.concatenate([own_block, pair_far + pair_owner * blocks])
    first_w = jnp.ones((blocks + pair_count,), jnp.float32)
    second_w = jnp.concatenate(
        [jnp.zeros((blocks,), jnp.float32), jnp.ones((pair_count,), jnp.float32)]
    )
    height = tables.shape[0]

    def settle(summed):
        return summed[:blocks] + to_next(summed[blocks:])

    def spread(values):
        return jnp.concatenate([values, from_next(values)], axis=0)

    density = settle(
        accumulate(density_tile, tables, first_idx, second_idx, first_w, second_w, height, 1)
    )[:, 0]
    (pressure_term, inverse), eos_back = jax.vjp(eos_state, density)
    pressure_pair = jnp.stack([pressure_term, inverse], axis=1)
    tables_two = jnp.concatenate([tables, spread(pressure_pair)], axis=1)
    acceleration = settle(
        accumulate(force_tile, tables_two, first_idx, second_idx, first_w, second_w, height, 3)
    )
    acceleration = acceleration + jnp.array([0.0, 0.0, -GRAVITY], jnp.float32)[None, :, None]
    new_v = velocity + DT * acceleration
    new_x = positions + DT * new_v
    grad_new_v = cot_v + DT * cot_x
    grad_two = settle(
        pull_back(
            force_tile,
            tables_two,
            first_idx,
            second_idx,
            first_w,
            second_w,
            spread(DT * grad_new_v),
        )
    )
    grad_density = eos_back((grad_two[:, 7], grad_two[:, 8]))[0]
    grad_one = settle(
        pull_back(
            density_tile,
            tables,
            first_idx,
            second_idx,
            first_w,
            second_w,
            spread(grad_density[:, None, :]),
        )
    )
    grad_x = cot_x + grad_two[:, 0:3] + grad_one[:, 0:3]
    grad_v = grad_new_v + grad_two[:, 3:6]
    grad_m = (grad_two[:, 6] + grad_one[:, 6]) * occupied
    return (new_x, new_v, grad_x, grad_v, grad_m)


def solution(mesh):
    placed = (
        P("slab", None, None),
        P("slab", None, None),
        P("slab", None),
        P("slab"),
        P("slab"),
        P("slab"),
        P("slab"),
        P("slab", None, None),
        P("slab", None, None),
    )
    return jax.shard_map(
        local,
        mesh=mesh,
        in_specs=placed,
        out_specs=(
            P("slab", None, None),
            P("slab", None, None),
            P("slab", None, None),
            P("slab", None, None),
            P("slab", None),
        ),
        check_vma=False,
    )
```

profile of v0, /device:TPU:6, one launch (start us, length us, event | category | flops | bytes accessed | tf_op | source)
XLA Modules:
  0.0 2183.8 jit_solution(17328395884100891173)
XLA Ops:
  3.9 8.1 collective-permute-start
  19.5 187.6 %while.40 = (s32[]{:T(128)}, f32[256,1,128]{2,0,1:T(8,128)S(1)}, s32[24,32]{1,0:T(8,128)}, f32[256,7,128]{2,1,0:T(8,128)S(1)}, s32[24,32]{1,0:T(8,128)}, /*index=5*/s32[]{:T(128)}, f32[]{:T(128)}, f32[24,32]{1,0:T(8,128)}) while((s32[]{:T(128)}, f32[256,1,128]{2,0,1:T(8,128)S(1)}, s32[24,32]{1,0:T(8,128)}, f32[256,7,128]{2,1,0:T(8,128)S(1)}, ...), condition=%wide.region_6.7_spmd, body=%wide.region_0.6_spmd.sunk | while | flops 8399074 | bytes 5384033 | solution.py:85
  209.1 8.0 collective-permute-start.4
  225.3 824.3 %while.42 = (s32[]{:T(128)}, f32[256,9,128]{2,1,0:T(8,128)}, s32[24,32]{1,0:T(8,128)}, f32[256,9,128]{2,1,0:T(8,128)S(1)}, s32[24,32]{1,0:T(8,128)}, /*index=5*/...) while((s32[]{:T(128)}, f32[256,9,128]{2,1,0:T(8,128)}, s32[24,32]{1,0:T(8,128)}, ...), condition=%wide.region_40.41_spmd, body=%wide.region_18.40_spmd.sunk | while | flops 63035584 | bytes 53962716 | solution.py:105
  238.8 5.6 multiply_reduce_fusion.28
  244.4 6.1 fusion.140
  273.2 5.6 multiply_reduce_fusion.28
  278.8 6.1 fusion.140
  307.5 5.6 multiply_reduce_fusion.28
  313.1 6.1 fusion.140
  341.8 5.6 multiply_reduce_fusion.28
  347.4 6.1 fusion.140
  376.2 5.6 multiply_reduce_fusion.28
  381.8 6.1 fusion.140
  410.5 5.6 multiply_reduce_fusion.28
  416.1 6.1 fusion.140
  444.9 5.6 multiply_reduce_fusion.28
  450.5 6.1 fusion.140
  479.2 5.6 multiply_reduce_fusion.28
  484.8 6.1 fusion.140
  513.6 5.6 multiply_reduce_fusion.28
  519.2 6.1 fusion.140
  547.9 5.6 multiply_reduce_fusion.28
  553.5 6.1 fusion.140
  582.3 5.6 multiply_reduce_fusion.28
  587.9 6.1 fusion.140
  616.7 5.6 multiply_reduce_fusion.28
  622.3 6.1 fusion.140
  651.0 5.6 multiply_reduce_fusion.28
  656.6 6.1 fusion.140
  691.0 6.1 fusion.140
  719.7 5.6 multiply_reduce_fusion.28
  725.3 6.1 fusion.140
  754.0 5.6 multiply_reduce_fusion.28
  759.6 6.1 fusion.140
  788.4 5.6 multiply_reduce_fusion.28
  794.0 6.1 fusion.140
  828.3 6.1 fusion.140
  862.7 6.1 fusion.140
  897.0 6.1 fusion.140
  931.4 6.1 fusion.140
  965.7 6.1 fusion.140
  1000.0 6.1 fusion.140
  1034.4 6.1 fusion.140
  1054.6 13.5 collective-permute-done.5
  1073.0 570.6 %while.43 = (s32[]{:T(128)}, f32[256,7,128]{2,1,0:T(8,128)S(1)}, s32[24,32]{1,0:T(8,128)}, f32[256,7,128]{2,1,0:T(8,128)}, s32[24,32]{1,0:T(8,128)}, /*index=5*/...) while((s32[]{:T(128)}, f32[256,7,128]{2,1,0:T(8,128)S(1)}, s32[24,32]{1,0:T(8,128)}, ...), condition=%wide.region_49.50_spmd, body=%wide.region_41.49_spmd.sunk | while | flops 23701696 | bytes 11825285 | solution.py:105
  1645.9 524.0 %while.41 = (s32[]{:T(128)}, f32[256,3,128]{2,1,0:T(4,128)S(1)}, s32[24,32]{1,0:T(8,128)}, f32[256,9,128]{2,1,0:T(8,128)}, s32[24,32]{1,0:T(8,128)}, /*index=5*/s32[]{:T(128)}, f32[24,32]{1,0:T(8,128)}) while((s32[]{:T(128)}, f32[256,3,128]{2,1,0:T(4,128)S(1)}, s32[24,32]{1,0:T(8,128)}, f32[256,9,128]{2,1,0:T(8,128)}, s32[24,32]{1,0:T(8,128)}, ...), condition=%wide.region_17.18_spmd, body=%wide.region_7.17_spmd.sunk | while | flops 25262304 | bytes 23504596 | solution.py:85
  2172.1 9.3 collective-permute-done.3
  (2638 shorter events, 1892.1 us)
Async XLA Ops:
  0.6 11.4 copy-start.20
  0.6 11.4 copy-start.21
  0.7 11.4 copy-start.22
  3.9 14.8 collective-permute-start
  19.0 190.1 %copy-start.11 = (f32[128,3,128]{2,0,1:T(8,128)S(1)}, f32[128,3,128]{2,0,1:T(8,128)}, u32[]{:S(2)}) copy-start(f32[128,3,128]{2,0,1:T(8,128)} %param.26) | copy-start | bytes 589828
  19.0 190.1 %copy-start.13 = (f32[128,3,128]{2,0,1:T(8,128)S(1)}, f32[128,3,128]{2,0,1:T(8,128)}, u32[]{:S(2)}) copy-start(f32[128,3,128]{2,0,1:T(8,128)} %param.25) | copy-start | bytes 589828
  207.1 16.0 copy-start.1
  207.1 16.0 copy-start.7
  207.1 10.0 collective-permute-start.1
  209.1 11.2 collective-permute-start.4
  217.2 4.9 collective-permute-start.2
  1052.4 16.6 copy-start.8
  1052.4 15.6 collective-permute-start.5
  1069.1 3.8 collective-permute-start.6
  1089.3 4.1 copy-start.19
  1089.4 5.8 copy-start.17
  1113.1 5.8 copy-start.17
  1136.9 5.8 copy-start.17
  1160.7 5.8 copy-start.17
  1184.4 5.8 copy-start.17
  1208.2 5.8 copy-start.17
  1232.0 5.8 copy-start.17
  1255.8 5.8 copy-start.17
  1279.5 5.8 copy-start.17
  1303.3 5.8 copy-start.17
  1327.1 5.8 copy-start.17
  1350.9 5.8 copy-start.17
  1374.7 5.8 copy-start.17
  1398.4 5.8 copy-start.17
  1422.2 5.8 copy-start.17
  1446.0 5.8 copy-start.17
  1469.8 5.8 copy-start.17
  1493.5 5.8 copy-start.17
  1517.3 5.8 copy-start.17
  1541.1 5.8 copy-start.17
  1564.9 5.8 copy-start.17
  1588.7 5.8 copy-start.17
  1612.4 5.8 copy-start.17
  1636.2 5.8 copy-start.17
  1643.9 538.4 %collective-permute-start.7 = (f32[128,7,128]{2,0,1:T(8,128)S(1)}, f32[128,7,128]{2,0,1:T(8,128)S(1)}, u32[]{:S(2)}, u32[]{:S(2)}) collective-permute-start(f32[128,7,128]{2,0,1:T(8,128)S(1)} %slice.212), channel_id=1, source_target_pairs={{0,1},{1,2},{2,3},{3,4},{4,5},{5,6},{6,7},{7,8},{8,9},{9,10},{10,1... | collective-permute-start | bytes 1376264 | tf_op jit(solution)/shard_map/ppermute | solution.py:19
  1645.9 535.5 %copy-start.9 = (f32[128,3,128]{2,0,1:T(8,128)S(1)}, f32[128,3,128]{2,0,1:T(8,128)}, u32[]{:S(2)}) copy-start(f32[128,3,128]{2,0,1:T(8,128)} %param.18) | copy-start | bytes 589828
  1645.9 535.5 %copy-start.10 = (f32[128,3,128]{2,0,1:T(8,128)S(1)}, f32[128,3,128]{2,0,1:T(8,128)}, u32[]{:S(2)}) copy-start(f32[128,3,128]{2,0,1:T(8,128)} %param.19) | copy-start | bytes 589828
  1645.9 535.5 %copy-start.24 = (f32[3]{0:T(128)S(1)}, f32[3]{0:T(128)}, u32[]{:S(2)}) copy-start(f32[3]{0:T(128)} %constant.131.clone) | copy-start | bytes 40
  2169.9 12.4 copy-start.4
  2169.9 12.4 copy-start.23
  2169.9 13.1 copy-start.12
  2170.0 13.1 copy-start.14
  2170.0 11.3 collective-permute-start.3
  (123 other events, 205.3 us)
where the time goes:
time: 2200 us; the launch traced here: 2180 us
  other arithmetic  1650 us (75%)
  local copies, waits for them, and re-layouts  458 us (21%)
  waiting for transfers between devices  32.2 us (1%)
  starting transfers between devices  28.5 us (1%)
    scatter-add x96, other arithmetic, pull_one_group(): gradient = gradient.at[lead_idx].add(grad_a).at[other_idx].add(grad_b)  272 us
    reduce_sum x48, other arithmetic, separation(): offsets = a[:, 0:3, :, None] - b[:, 0:3, None, :]  240 us
    reduce_sum x72, other arithmetic, separation(): return (offsets, jnp.sum(offsets * offsets, axis=1))  149 us
    reduce_sum x24, other arithmetic, force_tile(): push_a = pressure * b[:, 6, None, :]  134 us
    gather x96, local copies, waits for them, and re-layouts, accumulate_one_group(): to_a, to_b = tile_fn(table_in[lead_idx], table_in[other_idx])  132 us
    gather x96, local copies, waits for them, and re-layouts, pull_one_group(): _, backward = jax.vjp(tile_fn, table_in[lead_idx], table_in[other_idx])  114 us
    reduce_sum x24, other arithmetic, force_tile(): push_b[:, None] * offsets  113 us
    reduce_sum x24, other arithmetic, force_tile(): jnp.sum(push_b[:, None] * offsets, axis=2)  93.6 us
  transfers between devices with their start and end apart: 8, of which 6 were waited for; matrix products, arithmetic and copies ran while one was open for 24% of the time, Pallas kernels for 0%

commit v1 on v0

v1 whole, which is shorter than its diff:
```python
import functools

import jax
import jax.numpy as jnp
from jax import lax
from jax.experimental import pallas as pl
from jax.experimental.pallas import tpu as pltpu
from jax.sharding import PartitionSpec as P

DT = 0.1
GRAVITY = 1.0
KAPPA = 1.0 / 128.0
LEAD = 64
SHORT = 32
LONG = 16
F32 = jnp.float32
BF16 = jnp.bfloat16


def dot(a, b, ca=1, cb=0):
    return lax.dot_general(a, b, (((ca,), (cb,)), ((), ())), preferred_element_type=F32)


def rounded(value):
    return value.astype(BF16).astype(F32)


def halves(value):
    high = rounded(value)
    return high, value - high


def thirds(value):
    high = rounded(value)
    rest = value - high
    middle = rounded(rest)
    return high, middle, rest - middle


def source_features(e):
    h, m, l = thirds(e)
    return jnp.concatenate([h, h, m, h, l, m], axis=0).astype(BF16)


def target_features(r):
    h, m, l = thirds(r)
    return jnp.concatenate([h, m, h, l, h, m], axis=0).astype(BF16)


def row_index():
    return lax.broadcasted_iota(jnp.int32, (8, 128), 0)


def basis(a):
    return jnp.where(row_index() < 5, a, 0.0)


def target_basis(a):
    row = row_index()
    return jnp.where(
        row == 0, 1.0 - a[1:2], jnp.where(row == 1, -1.0, jnp.where(row < 5, 2.0 * a, 0.0))
    )


def list_kernel(home, far, owner, p_home, p_far, p_owner, entries, count):
    pairs = home.shape[0]
    blocks = 128
    dead = blocks * 512 + blocks

    def own(k, at):
        h, f, o = home[k], far[k], owner[k]
        entries[at] = h * 512 + f + blocks + o * blocks
        entries[at + 1] = f * 512 + h + blocks
        return at + 2 - o

    def previous(k, at):
        entries[at] = p_far[k] * 512 + p_home[k]
        return at + p_owner[k]

    def self_pair(b, at):
        entries[LEAD + b] = b * 512 + b + blocks
        return at

    lax.fori_loop(0, blocks, self_pair, 0, unroll=8)
    for extra in range(LEAD):
        entries[extra] = dead
    at = lax.fori_loop(0, pairs, own, LEAD + blocks, unroll=8)
    at = lax.fori_loop(0, pairs, previous, at, unroll=8)
    for extra in range(2 * LEAD):
        entries[at + extra] = dead
    count[0] = at - LEAD


def make_list(home, far, owner, p_home, p_far, p_owner):
    pairs = home.shape[0]
    smem = pl.BlockSpec(memory_space=pltpu.SMEM)
    return pl.pallas_call(
        list_kernel,
        out_shape=(
            jax.ShapeDtypeStruct((128 + 3 * pairs + 4 * LEAD,), jnp.int32),
            jax.ShapeDtypeStruct((8,), jnp.int32),
        ),
        in_specs=[smem] * 6,
        out_specs=(smem, smem),
        name="tile_list",
    )(home, far, owner, p_home, p_far, p_owner)


def group_at(entries, t, size):
    found = [entries[LEAD + t * size + k] for k in range(size)]
    return [(lax.shift_right_logical(e, 9), lax.bitwise_and(e, 511)) for e in found]


def group_loop(count, size, stages, step):
    groups = lax.shift_right_logical(count[0] + (size - 1), size.bit_length() - 1)

    def body(t, carry):
        step(t)
        return carry

    lax.fori_loop(0, groups + stages - 1, body, 0)


def two_tiles(sources, targets, one, two):
    (x0, y0), (x1, y1) = one, two
    lhs = jnp.concatenate([sources[y0], sources[y1]], axis=0)
    zero = jnp.zeros((48, 128), BF16)
    rhs = jnp.concatenate(
        [
            jnp.concatenate([targets[x0], zero], axis=1),
            jnp.concatenate([zero, targets[x1]], axis=1),
        ],
        axis=0,
    )
    return jnp.maximum(dot(lhs, rhs, 0, 0), 0.0)


def make_tiles(sources, targets, tiles, k, distances):
    distances[k // 2] = two_tiles(sources, targets, tiles[k], tiles[k + 1])


def for_blocks(blocks, fn, unroll=4):
    def body(b, carry):
        fn(b)
        return carry

    lax.fori_loop(0, blocks, body, 0, unroll=unroll)


def density_kernel(entries, count, a_prev, a_own, a_next, out, sources, targets, acc, distances):
    blocks = a_own.shape[0]
    for part, a_ref in enumerate((a_prev, a_own, a_next)):

        def prepare(b, part=part, a_ref=a_ref):
            a = a_ref[b]
            sources[part * blocks + b] = source_features(basis(a) * a[6:7])
            if part == 1:
                targets[b] = target_features(target_basis(a))
                acc[b] = jnp.zeros((8, 128), F32)

        for_blocks(blocks, prepare)
    targets[blocks] = jnp.zeros((48, 128), BF16)
    acc[blocks] = jnp.zeros((8, 128), F32)

    def step(t):
        newer, older = group_at(entries, t, SHORT), group_at(entries, t - 1, SHORT)
        for k in range(0, SHORT, 2):
            c = distances[k // 2]
            mass_kernel = c * c * c
            total = jnp.sum(mass_kernel.reshape(16, 8, 256), axis=0)
            for j in range(2):
                x = older[k + j][0]
                acc[x] = acc[x] + total[:, 128 * j : 128 * j + 128]
            make_tiles(sources, targets, newer, k, distances)

    group_loop(count, SHORT, 2, step)

    def finish(b):
        density = KAPPA * jnp.sum(acc[b], axis=0, keepdims=True)
        square = density * density + 0.25
        inverse = lax.rsqrt(square)
        inverse = inverse * (1.5 - 0.5 * square * inverse * inverse)
        bounded = square * inverse
        pressure = 0.5 * (bounded - inverse * inverse)
        row = lax.broadcasted_iota(jnp.int32, (4, 128), 0)
        out[b] = jnp.where(
            row == 0, pressure, jnp.where(row == 1, inverse, jnp.where(row == 2, density, bounded))
        )

    for_blocks(blocks, finish)


def run_density(entries, count, a_prev, a_own, a_next):
    blocks = a_own.shape[0]
    smem = pl.BlockSpec(memory_space=pltpu.SMEM)
    vmem = pl.BlockSpec(memory_space=pltpu.VMEM)
    return pl.pallas_call(
        density_kernel,
        out_shape=jax.ShapeDtypeStruct((blocks, 4, 128), F32),
        in_specs=[smem, smem, vmem, vmem, vmem],
        out_specs=vmem,
        scratch_shapes=[
            pltpu.VMEM((3 * blocks, 48, 128), BF16),
            pltpu.VMEM((blocks + 1, 48, 128), BF16),
            pltpu.VMEM((blocks + 1, 8, 128), F32),
            pltpu.VMEM((SHORT // 2, 128, 256), F32),
        ],
        compiler_params=pltpu.CompilerParams(vmem_limit_bytes=24 << 20),
        cost_estimate=pl.CostEstimate(flops=10**9, bytes_accessed=2 * 10**6, transcendentals=0),
        name="density",
    )(entries, count, a_prev, a_own, a_next)


F_ROWS = 72
C_ROWS = 64


def stacked(groups):
    value = jnp.concatenate(groups, axis=0)
    high, low = halves(value)
    return jnp.concatenate([high, low], axis=0).astype(BF16)


def split_rows(tile):
    high, low = halves(tile)
    return jnp.concatenate([high.astype(BF16), low.astype(BF16)], axis=0)


def matrix_sum(channels, right):
    both = dot(jnp.concatenate([channels, channels], axis=1), right)
    rows = channels.shape[0] // 2
    return both[:rows] + both[rows:]


def force_kernel(
    entries, count, a_prev, a_own, a_next, b_prev, b_own, b_next, q_prev, q_own, q_next,
    cot_x, out, h_out, sources, targets, f_channels, c_channels, acc,
    distances, f_right, c_right,
):
    blocks = a_own.shape[0]
    row = row_index()
    parts = ((a_prev, b_prev, q_prev), (a_own, b_own, q_own), (a_next, b_next, q_next))
    for part, (a_ref, b_ref, q_ref) in enumerate(parts):

        def prepare(b, part=part, a_ref=a_ref, b_ref=b_ref, q_ref=q_ref):
            at = part * blocks + b
            a = a_ref[b]
            vg_rows = b_ref[b]
            p, q = q_ref[b, 0:1], q_ref[b, 1:2]
            e = basis(a)
            x = [a[2 + k : 3 + k] for k in range(3)]
            v = [vg_rows[k : k + 1] for k in range(3)]
            g = [vg_rows[3 + k : 4 + k] for k in range(3)]
            mass = a[5:6]
            u = mass * q
            vg = v[0] * g[0] + v[1] * g[1] + v[2] * g[2]
            xg = x[0] * g[0] + x[1] * g[1] + x[2] * g[2]
            sources[at] = source_features(e)
            e_one = jnp.where(row == 5, p, e)
            e_two = jnp.where(
                row >= 5, p * pltpu.roll(e, 3, 0), jnp.where(row == 1, p, e)
            )
            f_channels[at] = stacked(
                [g[k] * e_one for k in range(3)]
                + [jnp.where(row == 5, p * xg, vg * e_one), u * e_one]
                + [(u * v[k]) * e_one for k in range(3)]
                + [mass * e_two]
            )
            me = mass * e_two
            c_channels[at] = stacked(
                [me] + [x[k] * me for k in range(3)] + [g[k] * e_two for k in range(3)]
                + [xg * e_two]
            )
            if part == 1:
                targets[b] = target_features(target_basis(a))
                acc[b] = jnp.zeros((F_ROWS + C_ROWS, 128), F32)

        for_blocks(blocks, prepare, unroll=2)
    targets[blocks] = jnp.zeros((48, 128), BF16)
    acc[blocks] = jnp.zeros((F_ROWS + C_ROWS, 128), F32)

    def step(t):
        newest, oldest = group_at(entries, t, LONG), group_at(entries, t - 2, LONG)
        for k in range(0, LONG, 2):
            for j in range(2):
                x, y = oldest[k + j]
                f_sum = matrix_sum(f_channels[y], f_right[k + j])
                c_sum = matrix_sum(c_channels[y], c_right[k + j])
                acc[x, 0:F_ROWS] = acc[x, 0:F_ROWS] + f_sum
                acc[x, F_ROWS : F_ROWS + C_ROWS] = acc[x, F_ROWS : F_ROWS + C_ROWS] + c_sum
            for j in range(2):
                c = distances[k // 2, :, 128 * j : 128 * j + 128]
                f_right[k + j] = split_rows(c * c)
                c_right[k + j] = split_rows(c)
            make_tiles(sources, targets, newest, k, distances)

    group_loop(count, LONG, 3, step)

    def finish(b):
        a = a_own[b]
        vg_rows = b_own[b]
        p, q = q_own[b, 0:1], q_own[b, 1:2]
        density, bounded = q_own[b, 2:3], q_own[b, 3:4]
        x = [a[2 + k : 3 + k] for k in range(3)]
        v = [vg_rows[k : k + 1] for k in range(3)]
        g = [vg_rows[3 + k : 4 + k] for k in range(3)]
        mass = a[5:6]
        u = mass * q
        vg = v[0] * g[0] + v[1] * g[1] + v[2] * g[2]
        xg = x[0] * g[0] + x[1] * g[1] + x[2] * g[2]
        r = target_basis(a)

        def group(k):
            return acc[b, 8 * k : 8 * k + 8]

        s_g = [group(k) for k in range(3)]
        s_vg, s_u = group(3), group(4)
        s_uv = [group(5 + k) for k in range(3)]
        s_m = group(8)
        c_m = group(9)
        c_mx = [group(10 + k) for k in range(3)]
        c_g = [group(13 + k) for k in range(3)]
        c_xg = group(16)

        def weighted(s):
            return jnp.sum(s * r, axis=0, keepdims=True)

        m0, m1 = s_m[0:1], s_m[1:2]
        mx = [s_m[2 + k : 3 + k] for k in range(3)]
        mpx = [s_m[5 + k : 6 + k] for k in range(3)]
        g0 = [s_g[k][0:1] for k in range(3)]
        g1 = [s_g[k][5:6] for k in range(3)]
        xg0 = s_g[0][2:3] + s_g[1][3:4] + s_g[2][4:5]
        xg1 = s_vg[5:6]
        xm = [x[k] * m0 - mx[k] for k in range(3)]
        energy = weighted(s_vg - (v[0] * s_g[0] + v[1] * s_g[1] + v[2] * s_g[2]))
        xdg0 = x[0] * g0[0] + x[1] * g0[1] + x[2] * g0[2]
        xdg1 = x[0] * g1[0] + x[1] * g1[1] + x[2] * g1[2]
        grad_m = KAPPA * (-6.0 * (p * (xdg0 - xg0) + xdg1 - xg1) - 0.5 * q * energy)
        grad_q = (-0.5 * KAPPA) * mass * energy
        grad_p = (6.0 * KAPPA) * (
            g[0] * xm[0] + g[1] * xm[1] + g[2] * xm[2] - mass * (xdg0 - xg0)
        )
        f_v = (
            u * (v[0] * s_g[0] + v[1] * s_g[1] + v[2] * s_g[2] - s_vg)
            + g[0] * s_uv[0] + g[1] * s_uv[1] + g[2] * s_uv[2] - vg * s_u
        )
        c_d = (
            xg * c_m - (g[0] * c_mx[0] + g[1] * c_mx[1] + g[2] * c_mx[2])
            + mass * (c_xg - (x[0] * c_g[0] + x[1] * c_g[1] + x[2] * c_g[2]))
        )
        c_d0 = p * c_d[0:1] + c_d[1:2]
        rows = []
        new_v, grad_v, grad_x = [], [], []
        for k in range(3):
            accel = KAPPA * (
                6.0 * (p * xm[k] + x[k] * m1 - mpx[k])
                + 0.5 * weighted(s_uv[k] - v[k] * s_u)
            )
            if k == 2:
                accel = accel - GRAVITY
            new_v.append(v[k] + DT * accel)
            grad_v.append(
                g[k] * (1.0 / DT) - (0.5 * KAPPA) * weighted(g[k] * s_u - u * s_g[k])
            )
            through = 24.0 * (
                x[k] * c_d0 - (p * c_d[2 + k : 3 + k] + c_d[5 + k : 6 + k])
            ) + 3.0 * (x[k] * f_v[0:1] - f_v[2 + k : 3 + k])
            direct = 6.0 * (g[k] * (p * m0 + m1) - mass * (p * g0[k] + g1[k]))
            grad_x.append(cot_x[b, k : k + 1] + KAPPA * (direct - through))
        new_x = [x[k] + DT * new_v[k] for k in range(3)]
        inv = q
        h = (density * inv) * (
            0.5 * (1.0 + 2.0 * inv * inv * inv) * grad_p - inv * inv * grad_q
        )
        rows = new_x + new_v + grad_v + grad_x + xm + [grad_m]
        for k, value in enumerate(rows):
            out[b, k : k + 1] = value
        h_out[b] = h

    for_blocks(blocks, finish, unroll=1)


def run_force(entries, count, a, b, q, cot_x):
    blocks = cot_x.shape[0]
    smem = pl.BlockSpec(memory_space=pltpu.SMEM)
    vmem = pl.BlockSpec(memory_space=pltpu.VMEM)
    return pl.pallas_call(
        force_kernel,
        out_shape=(
            jax.ShapeDtypeStruct((blocks, 16, 128), F32),
            jax.ShapeDtypeStruct((blocks, 1, 128), F32),
        ),
        in_specs=[smem, smem] + [vmem] * 10,
        out_specs=(vmem, vmem),
        scratch_shapes=[
            pltpu.VMEM((3 * blocks, 48, 128), BF16),
            pltpu.VMEM((blocks + 1, 48, 128), BF16),
            pltpu.VMEM((3 * blocks, 2 * F_ROWS, 128), BF16),
            pltpu.VMEM((3 * blocks, 2 * C_ROWS, 128), BF16),
            pltpu.VMEM((blocks + 1, F_ROWS + C_ROWS, 128), F32),
            pltpu.VMEM((LONG // 2, 128, 256), F32),
            pltpu.VMEM((LONG, 256, 128), BF16),
            pltpu.VMEM((LONG, 256, 128), BF16),
        ],
        compiler_params=pltpu.CompilerParams(vmem_limit_bytes=58 << 20),
        name="force",
    )(entries, count, *a, *b, *q, cot_x)


def adjoint_kernel(
    entries, count, a_prev, a_own, a_next, h_prev, h_own, h_next, partial, occupied,
    gx_out, gm_out, sources, targets, channels, acc, distances, right,
):
    blocks = a_own.shape[0]
    for part, (a_ref, h_ref) in enumerate(((a_prev, h_prev), (a_own, h_own), (a_next, h_next))):

        def prepare(b, part=part, a_ref=a_ref, h_ref=h_ref):
            at = part * blocks + b
            a = a_ref[b]
            e = basis(a)
            sources[at] = source_features(e)
            channels[at] = stacked([h_ref[b] * e])
            if part == 1:
                targets[b] = target_features(target_basis(a))
                acc[b] = jnp.zeros((8, 128), F32)

        for_blocks(blocks, prepare)
    targets[blocks] = jnp.zeros((48, 128), BF16)
    acc[blocks] = jnp.zeros((8, 128), F32)

    def step(t):
        newest, oldest = group_at(entries, t, SHORT), group_at(entries, t - 2, SHORT)
        for k in range(0, SHORT, 2):
            for j in range(2):
                x, y = oldest[k + j]
                acc[x] = acc[x] + matrix_sum(channels[y], right[k + j])
            for j in range(2):
                c = distances[k // 2, :, 128 * j : 128 * j + 128]
                right[k + j] = split_rows(c * c)
            make_tiles(sources, targets, newest, k, distances)

    group_loop(count, SHORT, 3, step)

    def finish(b):
        a = a_own[b]
        s = acc[b]
        h = h_own[b]
        mass = a[5:6]
        grad_m = partial[b, 15:16] + KAPPA * jnp.sum(s * target_basis(a), axis=0, keepdims=True)
        gm_out[b] = grad_m * occupied[b]
        for k in range(3):
            pull = h * partial[b, 12 + k : 13 + k] + mass * (
                a[2 + k : 3 + k] * s[0:1] - s[2 + k : 3 + k]
            )
            gx_out[b, k : k + 1] = partial[b, 9 + k : 10 + k] - (6.0 * KAPPA) * pull

    for_blocks(blocks, finish, unroll=2)


def run_adjoint(entries, count, a, h, partial, occupied):
    blocks = partial.shape[0]
    smem = pl.BlockSpec(memory_space=pltpu.SMEM)
    vmem = pl.BlockSpec(memory_space=pltpu.VMEM)
    return pl.pallas_call(
        adjoint_kernel,
        out_shape=(
            jax.ShapeDtypeStruct((blocks, 3, 128), F32),
            jax.ShapeDtypeStruct((blocks, 1, 128), F32),
        ),
        in_specs=[smem, smem] + [vmem] * 8,
        out_specs=(vmem, vmem),
        scratch_shapes=[
            pltpu.VMEM((3 * blocks, 48, 128), BF16),
            pltpu.VMEM((blocks + 1, 48, 128), BF16),
            pltpu.VMEM((3 * blocks, 16, 128), BF16),
            pltpu.VMEM((blocks + 1, 8, 128), F32),
            pltpu.VMEM((SHORT // 2, 128, 256), F32),
            pltpu.VMEM((SHORT, 256, 128), BF16),
        ],
        compiler_params=pltpu.CompilerParams(vmem_limit_bytes=24 << 20),
        name="adjoint",
    )(entries, count, *a, *h, partial, occupied)


def shifted(value, by):
    devices = lax.axis_size("slab")
    pairs = [(i, i + by) for i in range(devices) if 0 <= i + by < devices]
    return lax.ppermute(value, "slab", pairs)


def around(value):
    return shifted(value, 1), value, shifted(value, -1)


def cube_root(mass):
    safe = jnp.where(mass > 0.0, mass, 1.0)
    root = jnp.exp(jnp.log(safe) * (1.0 / 3.0))
    root = root - (root * root * root - safe) / (3.0 * root * root)
    return jnp.where(mass > 0.0, root, 0.0)


def local(positions, velocity, masses, counts, pair_home, pair_far, pair_owner, cot_x, cot_v):
    occupied = (lax.broadcasted_iota(jnp.int32, masses.shape, 1) < counts[:, None]).astype(F32)
    mass = (masses * occupied)[:, None, :]
    norm = jnp.sum(positions * positions, axis=1, keepdims=True)
    one = jnp.ones_like(norm)
    a_own = jnp.concatenate(
        [one, norm, positions, mass, cube_root(mass), jnp.zeros_like(norm)], axis=1
    )
    g = DT * (cot_v + DT * cot_x)
    b_own = jnp.concatenate([velocity, g, jnp.zeros_like(g[:, :2])], axis=1)
    table = jnp.stack([pair_home, pair_far, pair_owner])
    p_table = shifted(table, 1)
    a = around(a_own)
    b = around(b_own)
    entries, count = make_list(
        pair_home, pair_far, pair_owner, p_table[0], p_table[1], p_table[2]
    )
    state = run_density(entries, count, *a)
    pq = state[:, :2]
    q = (shifted(pq, 1), state, shifted(pq, -1))
    partial, h = run_force(entries, count, a, b, q, cot_x)
    grad_x, grad_m = run_adjoint(entries, count, a, around(h), partial, occupied[:, None, :])
    return (partial[:, 0:3], partial[:, 3:6], grad_x, partial[:, 6:9], grad_m[:, 0])


def solution(mesh):
    block = P("slab", None, None)
    flat = P("slab")
    return jax.shard_map(
        local,
        mesh=mesh,
        in_specs=(block, block, P("slab", None), flat, flat, flat, flat, block, block),
        out_specs=(block, block, block, block, P("slab", None)),
        check_vma=False,
    )
```

time: 2200 us -> 240 us (0.11)
  other arithmetic: 1650 us -> 1.52 us
  local copies, waits for them, and re-layouts: 458 us -> 11.1 us
  Pallas kernels: 0 us -> 169 us
  waiting for transfers between devices: 32.2 us -> 9.55 us
    reduce_sum x408 -> x1, other arithmetic: 1110 us -> 0.02 us  [local(): norm = jnp.sum(positions * positions, axis=1, keepdims=True)]
    scatter-add x192 -> x0, other arithmetic: 391 us -> none  [the longest x96 272 us: pull_one_group(): gradient = gradient.at[lead_idx].add(grad_a).at[other_idx].add(grad_b)]
    gather x288 -> x0, local copies, waits for them, and re-layouts: 320 us -> none  [the longest x96 132 us: accumulate_one_group(): to_a, to_b = tile_fn(table_in[lead_idx], table_in[other_idx])]
    pallas_call x0 -> x4, Pallas kernels: none -> 169 us  [the longest x1 98.9 us: run_force(): pl.pallas_call(force_kernel, out_shape=(jax.ShapeDtypeStruct((blocks, 16,...]
    select_n x96 -> x1, other arithmetic: 68.6 us -> 0.12 us  [cube_root(): return jnp.where(mass > 0.0, root, 0.0)]
    while x292 -> x0, local copies, waits for them, and re-layouts: 46.9 us -> none
    mul x315 -> x0, other arithmetic: 42.9 us -> none  [the longest x72 36.4 us: accumulate_one_group(): running = running.at[other_idx].add(to_b * other_w[:, None, None])]
    slice x340 -> x3, local copies, waits for them, and re-layouts: 43.4 us -> 2.55 us  [the longest x1 1.88 us: local(): partial[:, 6:9]]
  transfers between devices with their start and end apart: 8 -> 9, of which waited for: 6 -> 3; matrix products, arithmetic and copies ran while one was open for 24% -> 3% of each run, Pallas kernels for 0% -> 14%
where the time goes in v1:
time: 240 us; the launch traced here: 236 us
  Pallas kernels  169 us (70%)
  starting transfers between devices  43.5 us (18%)
  local copies, waits for them, and re-layouts  11.1 us (5%)
  waiting for transfers between devices  9.55 us (4%)
    pallas_call x1, Pallas kernels, run_force(): pl.pallas_call(force_kernel, out_shape=(jax.ShapeDtypeStruct((blocks, 16,...  98.9 us
    ppermute x9, starting transfers between devices, shifted(): return lax.ppermute(value, 'slab', pairs)  43.5 us
    pallas_call x1, Pallas kernels, run_adjoint(): pl.pallas_call(adjoint_kernel, out_shape=(jax.ShapeDtypeStruct((blocks, 3...  37.8 us
    pallas_call x1, Pallas kernels, run_density(): pl.pallas_call(density_kernel, out_shape=jax.ShapeDtypeStruct((blocks, 4,...  24.7 us
    ppermute x9, waiting for transfers between devices, shifted(): return lax.ppermute(value, 'slab', pairs)  9.55 us
    unnamed x60, local copies, waits for them, and re-layouts  7.74 us
    pallas_call x1, Pallas kernels, make_list(): pl.pallas_call(list_kernel, out_shape=(jax.ShapeDtypeStruct((128 + 3 * pa...  7.35 us
  transfers between devices with their start and end apart: 9, of which 3 were waited for; matrix products, arithmetic and copies ran while one was open for 3% of the time, Pallas kernels for 14%

profile of v1, /device:TPU:6, one launch (start us, length us, event | category | flops | bytes accessed | tf_op | source)
XLA Modules:
  0.0 235.6 jit_solution(4734754778006691691)
XLA Ops:
  0.6 1.1 copy.24
  1.8 0.0 copy-start.22
  1.8 0.0 copy-start.26
  1.8 0.8 copy-done.22
  2.6 0.1 compare_select_fusion
  2.8 0.0 copy-start.17
  2.9 0.0 copy-start.18
  2.9 0.7 concatenate.6.a_own
  3.5 0.0 copy-start.19
  3.5 2.1 collective-permute-start.1
  5.6 8.1 %collective-permute-start.2 = (f32[128,8,128]{2,1,0:T(8,128)S(1)}, f32[128,8,128]{2,1,0:T(8,128)S(1)}, u32[]{:S(2)}, u32[]{:S(2)}) collective-permute-start(f32[128,8,128]{2,1,0:T(8,128)S(1)} %concatenate.6.a_own), channel_id=1, source_target_pairs={{1,0},{2,1},{3,2},{4,3},{5,4},{6,5},{7,6},{8,7},{9,8},{10,9},{11,1... | collective-permute-start | bytes 1572872 | tf_op jit(solution)/shard_map/ppermute | solution.py:489
  13.7 1.0 fusion.7
  14.8 0.1 copy.30
  14.9 0.1 pad.2.clone
  15.0 0.1 maximum_maximum_fusion.b_own
  15.2 0.0 copy-start.24
  15.2 2.1 collective-permute-start.3
  17.2 7.9 %collective-permute-start.4 = (f32[128,8,128]{2,1,0:T(8,128)S(1)}, f32[128,8,128]{2,1,0:T(8,128)S(1)}, u32[]{:S(2)}, u32[]{:S(2)}) collective-permute-start(f32[128,8,128]{2,1,0:T(8,128)S(1)} %maximum_maximum_fusion.b_own), channel_id=1, source_target_pairs={{1,0},{2,1},{3,2},{4,3},{5,4},{6,5},{7,6},{8,7},{9,8},{10,9},{11,1... | collective-permute-start | bytes 1572872 | tf_op jit(solution)/shard_map/ppermute | solution.py:489
  25.1 0.0 copy-start.25
  25.1 0.7 copy-done.25
  25.8 1.9 collective-permute-start
  27.8 7.3 %collective-permute-done = s32[3,640]{1,0:T(4,128)S(1)} collective-permute-done((s32[3,640]{1,0:T(4,128)S(1)}, s32[3,640]{1,0:T(4,128)S(1)}, u32[]{:S(2)}, u32[]{:S(2)}) %collective-permute-start) | collective-permute-done | bytes 7712 | tf_op jit(solution)/shard_map/ppermute | solution.py:489
  35.0 0.6 slice_reduce_fusion
  35.7 7.3 %tile_list.1 = (s32[2304]{0:T(1024)}, s32[8]{0:T(128)}) custom-call(s32[640]{0:T(1024)} %home.1, s32[640]{0:T(1024)} %far.1, s32[640]{0:T(1024)} %owner.1, s32[640]{0:T(1024)} %get-tuple-element.29.p_home, s32[640]{0:T(1024)} %get-tuple-element.28.p_far, s32[640]{0:T(1024)} %get-tuple-element.27.p_owner), custom_call_target="tpu_custom_call" | custom-call | tf_op jit(solution)/shard_map/tile_list/pallas_call | solution.py:97
  43.0 0.0 collective-permute-done.1.a_prev
  43.0 0.0 collective-permute-done.2.a_next
  43.1 0.7 copy-done.11
  43.7 0.7 copy-done.9
  44.5 24.7 %density.1.q_own = f32[128,4,128]{2,1,0:T(4,128)S(1)} custom-call(s32[2304]{0:T(1024)S(1)} %copy-done.9, s32[8]{0:T(128)S(1)} %copy-done.11, f32[128,8,128]{2,1,0:T(8,128)S(1)} %collective-permute-done.1.a_prev, f32[128,8,128]{2,1,0:T(8,128)S(1)} %concatenate.6.a_own, f32[128,8,128]{2,1,0:T(8,128)S(1)} %collective-permute-done.2.a_next), custom_call_target="tpu_custom_call" | custom-call | flops 1000000000 | bytes 2000000 | tf_op jit(solution)/shard_map/density/pallas_call | solution.py:197
  69.3 1.9 collective-permute-start.5
  71.2 7.9 %collective-permute-start.6 = (f32[128,2,128]{2,1,0:T(2,128)S(1)}, f32[128,2,128]{2,1,0:T(2,128)S(1)}, u32[]{:S(2)}, u32[]{:S(2)}) collective-permute-start(f32[128,2,128]{2,1,0:T(2,128)S(1)} %slice.31), channel_id=1, source_target_pairs={{1,0},{2,1},{3,2},{4,3},{5,4},{6,5},{7,6},{8,7},{9,8},{10,9},{11,1... | collective-permute-start | bytes 393224 | tf_op jit(solution)/shard_map/ppermute | solution.py:489
  79.1 0.2 compare_convert_fusion.occupied
  79.3 0.0 collective-permute-done.3.b_prev
  79.3 0.0 collective-permute-done.4.b_next
  79.3 0.5 collective-permute-done.5.q_prev
  79.8 1.8 collective-permute-done.6.q_next
  81.6 0.6 copy-done.21
  82.2 98.9 %force.1 = (f32[128,16,128]{2,1,0:T(8,128)}, f32[128,1,128]{2,1,0:T(1,128)}) custom-call(s32[2304]{0:T(1024)} %get-tuple-element.11.entries, s32[8]{0:T(128)} %get-tuple-element.12.count, f32[128,8,128]{2,1,0:T(8,128)} %copy-done.3, f32[128,8,128]{2,1,0:T(8,128)} %copy-done, f32[128,8,128]{2,1,0:T(8,128)} %copy-done.5, f32[128,8,128]{2,1,0:T(8,128)} %copy-done.15, ...), custom_call_target="tpu_custom_call" | custom-call | tf_op jit(solution)/shard_map/force/pallas_call | solution.py:388
  181.2 1.9 collective-permute-start.7
  183.1 9.8 %collective-permute-start.8 = (f32[128,1,128]{2,1,0:T(1,128)}, f32[128,1,128]{2,1,0:T(1,128)S(1)}, u32[]{:S(2)}, u32[]{:S(2)}) collective-permute-start(f32[128,1,128]{2,1,0:T(1,128)} %get-tuple-element.14.h_own), channel_id=1, source_target_pairs={{1,0},{2,1},{3,2},{4,3},{5,4},{6,5},{7,6},{8,7},{9,8},{10,9},{11,1... | collective-permute-start | bytes 196616 | tf_op jit(solution)/shard_map/ppermute | solution.py:489
  192.9 1.9 fusion.6
  194.8 0.7 copy.32
  195.5 0.7 copy.33
  196.2 0.7 copy.35
  196.9 0.0 collective-permute-done.8.h_next
  197.0 0.1 copy-done.8
  197.1 37.8 %adjoint.1 = (f32[128,3,128]{2,1,0:T(4,128)S(1)}, f32[128,1,128]{2,1,0:T(1,128)}) custom-call(s32[2304]{0:T(1024)S(1)} %copy-done.10, s32[8]{0:T(128)S(1)} %copy-done.12, f32[128,8,128]{2,1,0:T(8,128)S(1)} %copy-done.4, f32[128,8,128]{2,1,0:T(8,128)S(1)} %copy-done.1, f32[128,8,128]{2,1,0:T(8,128)S(1)} %copy-done.6, ...), custom_call_target="tpu_custom_call" | custom-call | tf_op jit(solution)/shard_map/adjoint/pallas_call | solution.py:465
  234.9 0.7 copy.34
  (51 shorter events, 0.2 us)
Async XLA Ops:
  0.6 1.1 copy-start.14
  1.8 0.8 copy-start.22
  1.8 0.8 copy-start.26
  2.8 10.9 %copy-start.17 = (f32[128,3,128]{2,0,1:T(8,128)S(1)}, f32[128,3,128]{2,0,1:T(8,128)}, u32[]{:S(2)}) copy-start(f32[128,3,128]{2,0,1:T(8,128)} %param.16) | copy-start | bytes 589828
  2.9 10.9 %copy-start.18 = (f32[128,3,128]{2,0,1:T(8,128)S(1)}, f32[128,3,128]{2,0,1:T(8,128)}, u32[]{:S(2)}) copy-start(f32[128,3,128]{2,0,1:T(8,128)} %param.17) | copy-start | bytes 589828
  3.5 39.5 %copy-start = (f32[128,8,128]{2,1,0:T(8,128)}, f32[128,8,128]{2,1,0:T(8,128)S(1)}, u32[]{:S(2)}) copy-start(f32[128,8,128]{2,1,0:T(8,128)S(1)} %concatenate.6.a_own) | copy-start | bytes 1572868
  3.5 11.2 %copy-start.19 = (f32[128,3,128]{2,0,1:T(8,128)S(1)}, f32[128,3,128]{2,0,1:T(8,128)}, u32[]{:S(2)}) copy-start(f32[128,3,128]{2,0,1:T(8,128)} %param.10) | copy-start | bytes 589828
  3.5 39.5 %collective-permute-start.1 = (f32[128,8,128]{2,1,0:T(8,128)S(1)}, f32[128,8,128]{2,1,0:T(8,128)S(1)}, u32[]{:S(2)}, u32[]{:S(2)}) collective-permute-start(f32[128,8,128]{2,1,0:T(8,128)S(1)} %concatenate.6.a_own), channel_id=1, source_target_pairs={{0,1},{1,2},{2,3},{3,4},{4,5},{5,6},{6,7},{7,8},{8,9},{9,10},{10,1... | collective-permute-start | bytes 1572872 | tf_op jit(solution)/shard_map/ppermute | solution.py:489
  5.6 37.4 %collective-permute-start.2 = (f32[128,8,128]{2,1,0:T(8,128)S(1)}, f32[128,8,128]{2,1,0:T(8,128)S(1)}, u32[]{:S(2)}, u32[]{:S(2)}) collective-permute-start(f32[128,8,128]{2,1,0:T(8,128)S(1)} %concatenate.6.a_own), channel_id=1, source_target_pairs={{1,0},{2,1},{3,2},{4,3},{5,4},{6,5},{7,6},{8,7},{9,8},{10,9},{11,1... | collective-permute-start | bytes 1572872 | tf_op jit(solution)/shard_map/ppermute | solution.py:489
  15.0 10.1 %copy-start.23 = (s32[640]{0:T(1024)S(1)}, s32[640]{0:T(1024)}, u32[]{:S(2)}) copy-start(s32[640]{0:T(1024)} %home.1) | copy-start | bytes 7684
  15.1 54.1 %copy-start.13 = (f32[128,8,128]{2,1,0:T(8,128)}, f32[128,8,128]{2,1,0:T(8,128)S(1)}, u32[]{:S(2)}) copy-start(f32[128,8,128]{2,1,0:T(8,128)S(1)} %maximum_maximum_fusion.b_own) | copy-start | bytes 1572868
  15.2 10.0 %copy-start.24 = (s32[640]{0:T(1024)S(1)}, s32[640]{0:T(1024)}, u32[]{:S(2)}) copy-start(s32[640]{0:T(1024)} %far.1) | copy-start | bytes 7684
  15.2 64.1 %collective-permute-start.3 = (f32[128,8,128]{2,1,0:T(8,128)S(1)}, f32[128,8,128]{2,1,0:T(8,128)S(1)}, u32[]{:S(2)}, u32[]{:S(2)}) collective-permute-start(f32[128,8,128]{2,1,0:T(8,128)S(1)} %maximum_maximum_fusion.b_own), channel_id=1, source_target_pairs={{0,1},{1,2},{2,3},{3,4},{4,5},{5,6},{6,7},{7,8},{8,9},{9,10},{10,1... | collective-permute-start | bytes 1572872 | tf_op jit(solution)/shard_map/ppermute | solution.py:489
  17.2 62.1 %collective-permute-start.4 = (f32[128,8,128]{2,1,0:T(8,128)S(1)}, f32[128,8,128]{2,1,0:T(8,128)S(1)}, u32[]{:S(2)}, u32[]{:S(2)}) collective-permute-start(f32[128,8,128]{2,1,0:T(8,128)S(1)} %maximum_maximum_fusion.b_own), channel_id=1, source_target_pairs={{1,0},{2,1},{3,2},{4,3},{5,4},{6,5},{7,6},{8,7},{9,8},{10,9},{11,1... | collective-permute-start | bytes 1572872 | tf_op jit(solution)/shard_map/ppermute | solution.py:489
  25.1 0.7 copy-start.25
  25.8 9.2 %collective-permute-start = (s32[3,640]{1,0:T(4,128)S(1)}, s32[3,640]{1,0:T(4,128)S(1)}, u32[]{:S(2)}, u32[]{:S(2)}) collective-permute-start(s32[3,640]{1,0:T(4,128)S(1)} %pad_add_fusion), channel_id=1, source_target_pairs={{0,1},{1,2},{2,3},{3,4},{4,5},{5,6},{6,7},{7,8},{8,9},{9,10},{10,1... | collective-permute-start | bytes 23048 | tf_op jit(solution)/shard_map/ppermute | solution.py:489
  43.0 26.2 %copy-start.3 = (f32[128,8,128]{2,1,0:T(8,128)}, f32[128,8,128]{2,1,0:T(8,128)S(1)}, u32[]{:S(2)}) copy-start(f32[128,8,128]{2,1,0:T(8,128)S(1)} %collective-permute-done.1.a_prev) | copy-start | bytes 1572868
  43.1 26.2 %copy-start.5 = (f32[128,8,128]{2,1,0:T(8,128)}, f32[128,8,128]{2,1,0:T(8,128)S(1)}, u32[]{:S(2)}) copy-start(f32[128,8,128]{2,1,0:T(8,128)S(1)} %collective-permute-done.2.a_next) | copy-start | bytes 1572868
  43.1 0.7 copy-start.11
  43.7 0.7 copy-start.9
  69.2 12.4 %copy-start.7 = (f32[128,4,128]{2,1,0:T(4,128)}, f32[128,4,128]{2,1,0:T(4,128)S(1)}, u32[]{:S(2)}) copy-start(f32[128,4,128]{2,1,0:T(4,128)S(1)} %density.1.q_own) | copy-start | bytes 786436
  69.3 10.5 %collective-permute-start.5 = (f32[128,2,128]{2,1,0:T(2,128)S(1)}, f32[128,2,128]{2,1,0:T(2,128)S(1)}, u32[]{:S(2)}, u32[]{:S(2)}) collective-permute-start(f32[128,2,128]{2,1,0:T(2,128)S(1)} %slice.31), channel_id=1, source_target_pairs={{0,1},{1,2},{2,3},{3,4},{4,5},{5,6},{6,7},{7,8},{8,9},{9,10},{10,1... | collective-permute-start | bytes 393224 | tf_op jit(solution)/shard_map/ppermute | solution.py:489
  71.2 10.4 %collective-permute-start.6 = (f32[128,2,128]{2,1,0:T(2,128)S(1)}, f32[128,2,128]{2,1,0:T(2,128)S(1)}, u32[]{:S(2)}, u32[]{:S(2)}) collective-permute-start(f32[128,2,128]{2,1,0:T(2,128)S(1)} %slice.31), channel_id=1, source_target_pairs={{1,0},{2,1},{3,2},{4,3},{5,4},{6,5},{7,6},{8,7},{9,8},{10,9},{11,1... | collective-permute-start | bytes 393224 | tf_op jit(solution)/shard_map/ppermute | solution.py:489
  79.3 2.3 copy-start.15
  79.3 2.3 copy-start.16
  79.8 1.8 copy-start.20
  81.6 0.7 copy-start.21
  181.2 15.8 %collective-permute-start.7 = (f32[128,1,128]{2,1,0:T(1,128)}, f32[128,1,128]{2,1,0:T(1,128)S(1)}, u32[]{:S(2)}, u32[]{:S(2)}) collective-permute-start(f32[128,1,128]{2,1,0:T(1,128)} %get-tuple-element.14.h_own), channel_id=1, source_target_pairs={{0,1},{1,2},{2,3},{3,4},{4,5},{5,6},{6,7},{7,8},{8,9},{9,10},{10,1... | collective-permute-start | bytes 196616 | tf_op jit(solution)/shard_map/ppermute | solution.py:489
  183.1 13.9 %collective-permute-start.8 = (f32[128,1,128]{2,1,0:T(1,128)}, f32[128,1,128]{2,1,0:T(1,128)S(1)}, u32[]{:S(2)}, u32[]{:S(2)}) collective-permute-start(f32[128,1,128]{2,1,0:T(1,128)} %get-tuple-element.14.h_own), channel_id=1, source_target_pairs={{1,0},{2,1},{3,2},{4,3},{5,4},{6,5},{7,6},{8,7},{9,8},{10,9},{11,1... | collective-permute-start | bytes 196616 | tf_op jit(solution)/shard_map/ppermute | solution.py:489
  192.9 4.0 %copy-start.2 = (f32[128,16,128]{2,1,0:T(8,128)S(1)}, f32[128,16,128]{2,1,0:T(8,128)}, u32[]{:S(2)}) copy-start(f32[128,16,128]{2,1,0:T(8,128)} %get-tuple-element.13.partial) | copy-start | bytes 3145732
  192.9 4.0 %copy-start.6 = (f32[128,8,128]{2,1,0:T(8,128)S(1)}, f32[128,8,128]{2,1,0:T(8,128)}, u32[]{:S(2)}) copy-start(f32[128,8,128]{2,1,0:T(8,128)} %copy-done.5) | copy-start | bytes 1572868
  194.8 2.1 copy-start.4
  195.5 1.4 copy-start.1
  196.2 0.9 copy-start.8
  196.2 0.9 copy-start.10
  196.2 0.9 copy-start.12

commit v2 on v1

v2 whole, which is shorter than its diff:
```python
import functools

import jax
import jax.numpy as jnp
from jax import lax
from jax.experimental import pallas as pl
from jax.experimental.pallas import tpu as pltpu
from jax.sharding import PartitionSpec as P

DT = 0.1
GRAVITY = 1.0
KAPPA = 1.0 / 128.0
LEAD = 64
SHORT = 32
LONG = 32
F32 = jnp.float32
BF16 = jnp.bfloat16


def dot(a, b, ca=1, cb=0):
    return lax.dot_general(a, b, (((ca,), (cb,)), ((), ())), preferred_element_type=F32)


def rounded(value):
    return value.astype(BF16).astype(F32)


def halves(value):
    high = rounded(value)
    return high, value - high


def thirds(value):
    high = rounded(value)
    rest = value - high
    middle = rounded(rest)
    return high, middle, rest - middle


def source_features(e):
    h, m, l = thirds(e)
    return jnp.concatenate([h, h, m, h, l, m], axis=0).astype(BF16)


def target_features(r):
    h, m, l = thirds(r)
    return jnp.concatenate([h, m, h, l, h, m], axis=0).astype(BF16)


def row_index():
    return lax.broadcasted_iota(jnp.int32, (8, 128), 0)


def basis(a):
    return jnp.where(row_index() < 5, a, 0.0)


def target_basis(a):
    row = row_index()
    return jnp.where(
        row == 0, 1.0 - a[1:2], jnp.where(row == 1, -1.0, jnp.where(row < 5, 2.0 * a, 0.0))
    )


DEAD = 128 * 512 + 128


def tile_lists(home, far, owner):
    blocks, pairs = 128, home.shape[0]
    own = jnp.arange(blocks, dtype=jnp.int32)
    receiver = jnp.concatenate([own, home, far])
    key = jnp.concatenate(
        [own + blocks, far + blocks * (1 + owner), home + jnp.where(owner == 0, 1, 3) * blocks]
    )
    here = key < 3 * blocks
    order = jnp.arange(key.shape[0], dtype=jnp.int32)
    same = key[:, None] == key[None, :]
    less = key[None, :] < key[:, None]

    def count(mask):
        return jnp.sum(mask.astype(jnp.int32), axis=1)

    rank = count(same & (order[None, :] < order[:, None]))
    odd = (rank == 0) & (count(same) % 2 == 1)
    place = count(less) + rank + count(less & odd[None, :])
    size = jnp.sum((here & odd).astype(jnp.int32) + here.astype(jnp.int32))
    away = ~here
    size_away = jnp.sum((away & odd).astype(jnp.int32) + away.astype(jnp.int32))

    def placed(slots, start, value, default):
        slot = jnp.arange(slots, dtype=jnp.int32)
        hit = (place - start)[None, :] == slot[:, None]
        return default + jnp.sum(jnp.where(hit, (value - default)[None, :], 0), axis=1)

    capacity = blocks + 2 * pairs + 2 * blocks
    mine = placed(capacity, 0, jnp.where(here, receiver * 512 + key, DEAD), DEAD)
    away_slots = pairs + blocks
    theirs = jnp.stack(
        [
            placed(away_slots, size, receiver, 128),
            placed(away_slots, size, key - 3 * blocks, 128),
            jnp.broadcast_to(size_away, (away_slots,)),
        ]
    )
    return mine, size, theirs


def whole_list(mine, size, previous):
    codes = previous[0] * 512 + previous[1]
    tail = jnp.full((codes.shape[0] + 2 * LEAD,), DEAD, jnp.int32)
    entries = jnp.concatenate([tail[:LEAD], mine, tail])
    entries = lax.dynamic_update_slice(entries, codes, (LEAD + size,))
    return entries, jnp.broadcast_to(size + previous[2, 0], (8,))


def group_at(entries, t, size):
    twos = []
    for k in range(0, size, 2):
        first = entries[LEAD + t * size + k]
        second = entries[LEAD + t * size + k + 1]
        twos.append(
            (
                lax.shift_right_logical(first, 9),
                lax.shift_right_logical(second, 9),
                lax.bitwise_and(first, 511),
            )
        )
    return twos


def group_loop(count, size, stages, buffers, step):
    groups = lax.shift_right_logical(count[0] + (size - 1), size.bit_length() - 1)
    even, odd = buffers

    def body(half, carry):
        step(2 * half, even, odd)

        @pl.when(groups > 0)
        def _():
            step(2 * half + 1, odd, even)

        return carry

    lax.fori_loop(0, lax.shift_right_logical(groups + stages, 1), body, 0)


def make_tiles(sources, targets, two, distances, k):
    x0, x1, y = two
    right = jnp.concatenate([targets[x0], targets[x1]], axis=1)
    distances[k] = jnp.maximum(dot(sources[y], right, 0, 0), 0.0)


def add_both(acc, two, rows, total):
    acc[two[0], rows] = acc[two[0], rows] + total[:, :128]
    acc[two[1], rows] = acc[two[1], rows] + total[:, 128:]


def for_blocks(blocks, fn, unroll=4):
    def body(b, carry):
        fn(b)
        return carry

    lax.fori_loop(0, blocks, body, 0, unroll=unroll)


def density_kernel(
    entries, count, a_prev, a_own, a_next, out, rho_out, sources, targets, acc, *distances,
):
    blocks = a_own.shape[0]

    def prepare(b):
        for part, a_ref in enumerate((a_prev, a_own, a_next)):
            a = a_ref[b]
            sources[part * blocks + b] = source_features(basis(a) * a[6:7])
            if part == 1:
                targets[b] = target_features(target_basis(a))
                acc[b] = jnp.zeros((8, 128), F32)

    for_blocks(blocks, prepare, unroll=4)
    targets[blocks] = jnp.zeros((48, 128), BF16)
    acc[blocks] = jnp.zeros((8, 128), F32)

    def step(t, now, later):
        newer, older = group_at(entries, t, SHORT), group_at(entries, t - 1, SHORT)
        for k in range(SHORT // 2):
            c = now[k]
            mass_kernel = c * c * c
            total = jnp.sum(mass_kernel.reshape(16, 8, 256), axis=0)
            add_both(acc, older[k], slice(0, 8), total)
            make_tiles(sources, targets, newer[k], later, k)

    group_loop(count, SHORT, 2, distances, step)

    def finish(b):
        density = KAPPA * jnp.sum(acc[b], axis=0, keepdims=True)
        square = density * density + 0.25
        inverse = lax.rsqrt(square)
        inverse = inverse * (1.5 - 0.5 * square * inverse * inverse)
        bounded = square * inverse
        pressure = 0.5 * (bounded - inverse * inverse)
        out[b, 0:1] = pressure
        out[b, 1:2] = inverse
        rho_out[b] = density

    for_blocks(blocks, finish, unroll=8)


def run_density(entries, count, a_prev, a_own, a_next):
    blocks = a_own.shape[0]
    smem = pl.BlockSpec(memory_space=pltpu.SMEM)
    vmem = pl.BlockSpec(memory_space=pltpu.VMEM)
    return pl.pallas_call(
        density_kernel,
        out_shape=(
            jax.ShapeDtypeStruct((blocks, 2, 128), F32),
            jax.ShapeDtypeStruct((blocks, 1, 128), F32),
        ),
        in_specs=[smem, smem, vmem, vmem, vmem],
        out_specs=(vmem, vmem),
        scratch_shapes=[
            pltpu.VMEM((3 * blocks, 48, 128), BF16),
            pltpu.VMEM((blocks + 1, 48, 128), BF16),
            pltpu.VMEM((blocks + 1, 8, 128), F32),
        ]
        + [pltpu.VMEM((SHORT // 2, 128, 256), F32)] * 2,
        compiler_params=pltpu.CompilerParams(vmem_limit_bytes=58 << 20),
        name="density",
    )(entries, count, a_prev, a_own, a_next)


F_ROWS = 56
C_ROWS = 64


def stacked(groups):
    value = jnp.concatenate(groups, axis=0)
    high, low = halves(value)
    return jnp.concatenate([high, low], axis=0).astype(BF16)


def split_into(rights, distances, k, powers):
    for start in range(0, 128, 16):
        rows = slice(start, start + 16)
        c = distances[k, rows]
        for right, power in zip(rights, powers):
            value = c if power == 1 else c * c
            high = value.astype(BF16)
            right[k, rows] = high
            right[k, 128 + start : 144 + start] = (value - high.astype(F32)).astype(BF16)


def matrix_sum(channels, right):
    both = dot(jnp.concatenate([channels, channels], axis=1), right)
    rows = channels.shape[0] // 2
    return both[:rows] + both[rows:]


def pair_basis(a, p):
    row = row_index()
    e = basis(a)
    return jnp.where(row >= 5, p * pltpu.roll(e, 3, 0), jnp.where(row == 1, p, e))


def force_channels(a, b, p, q):
    row = row_index()
    x = [a[2 + k : 3 + k] for k in range(3)]
    mass, xg = a[5:6], a[7:8]
    first = jnp.where(row >= 4, (mass * q) * b, b)
    with_p = jnp.where(row < 3, p * b, jnp.where(row == 3, p * xg, 0.0))
    second = jnp.where(
        row == 0,
        mass,
        jnp.where(
            row < 4, mass * pltpu.roll(a, 7, 0), jnp.where(row < 7, pltpu.roll(b, 4, 0), xg)
        ),
    )
    second_p = p * second
    f = [first, a[1:2] * first] + [x[k] * first for k in range(3)]
    f += [mass * pair_basis(a, p), with_p]
    c = [second] + [x[k] * second for k in range(3)]
    c += [second_p] + [x[k] * second_p for k in range(3)]
    return stacked(f), stacked(c)


def force_kernel(
    entries, count, a_prev, a_own, a_next, b_prev, b_own, b_next, q_prev, q_own, q_next,
    rho, cot_x, x_out, v_out, gv_out, out, h_out, sources, targets, f_channels, c_channels, acc,
    *buffers,
):
    blocks = a_own.shape[0]
    row = row_index()
    parts = ((a_prev, b_prev, q_prev), (a_own, b_own, q_own), (a_next, b_next, q_next))

    def prepare(b):
        for part, (a_ref, b_ref, q_ref) in enumerate(parts):
            at = part * blocks + b
            a = a_ref[b]
            sources[at] = source_features(basis(a))
            f, c = force_channels(a, b_ref[b], q_ref[b, 0:1], q_ref[b, 1:2])
            f_channels[at] = f
            c_channels[at] = c
            if part == 1:
                targets[b] = target_features(target_basis(a))
                acc[b] = jnp.zeros((F_ROWS + C_ROWS, 128), F32)

    for_blocks(blocks, prepare, unroll=2)
    targets[blocks] = jnp.zeros((48, 128), BF16)
    acc[blocks] = jnp.zeros((F_ROWS + C_ROWS, 128), F32)

    def step(t, now, later):
        newest, oldest = group_at(entries, t, LONG), group_at(entries, t - 2, LONG)
        for k in range(LONG // 2):
            y = oldest[k][2]
            add_both(acc, oldest[k], slice(0, F_ROWS), matrix_sum(f_channels[y], now[1][k]))
            add_both(
                acc, oldest[k], slice(F_ROWS, F_ROWS + C_ROWS),
                matrix_sum(c_channels[y], now[2][k]),
            )
            split_into(later[1:], now[0], k, (2, 1))
            make_tiles(sources, targets, newest[k], later[0], k)

    group_loop(count, LONG, 3, (buffers[:3], buffers[3:]), step)

    def finish(b):
        a = a_own[b]
        bb = b_own[b]
        p, q = q_own[b, 0:1], q_own[b, 1:2]
        n = a[1:2]
        x = [a[2 + k : 3 + k] for k in range(3)]
        g = [bb[k : k + 1] for k in range(3)]
        v = [bb[5 + k : 6 + k] for k in range(3)]
        vg = bb[3:4]
        mass, xg = a[5:6], a[7:8]
        u = mass * q

        def group(k):
            return acc[b, 8 * k : 8 * k + 8]

        s_one, s_n = group(0), group(1)
        s_x = [group(2 + k) for k in range(3)]
        s_m, s_p = group(5), group(6)
        c_one, c_p = group(7), group(11)
        c_x = [group(8 + k) for k in range(3)]
        c_px = [group(12 + k) for k in range(3)]

        weighted = (
            (1.0 - n) * s_one - s_n + 2.0 * (x[0] * s_x[0] + x[1] * s_x[1] + x[2] * s_x[2])
        )
        w_g = [weighted[k : k + 1] for k in range(3)]
        w_u = weighted[4:5]
        energy = weighted[3:4] - (v[0] * w_g[0] + v[1] * w_g[1] + v[2] * w_g[2])
        m0, m1 = s_m[0:1], s_m[1:2]
        xm = [x[k] * m0 - s_m[2 + k : 3 + k] for k in range(3)]
        g0 = [s_one[k : k + 1] for k in range(3)]
        g1 = [s_p[k : k + 1] for k in range(3)]
        xg0 = s_x[0][0:1] + s_x[1][1:2] + s_x[2][2:3]
        xdg0 = x[0] * g0[0] + x[1] * g0[1] + x[2] * g0[2] - xg0
        xdg1 = x[0] * g1[0] + x[1] * g1[1] + x[2] * g1[2] - s_p[3:4]
        grad_m = KAPPA * (-6.0 * (p * xdg0 + xdg1) - 0.5 * q * energy)
        grad_q = (-0.5 * KAPPA) * mass * energy
        grad_p = (6.0 * KAPPA) * (g[0] * xm[0] + g[1] * xm[1] + g[2] * xm[2] - mass * xdg0)
        c_weight = 24.0 * jnp.where(
            row == 0,
            xg,
            jnp.where(
                row < 4,
                -pltpu.roll(bb, 1, 0),
                jnp.where(row < 7, -mass * pltpu.roll(a, 2, 0), mass),
            ),
        )
        f_weight = 3.0 * jnp.where(
            row < 3,
            u * pltpu.roll(bb, 3, 0),
            jnp.where(row == 3, -u, jnp.where(row == 4, -vg, pltpu.roll(bb, 5, 0))),
        )

        def through(c_sum, cp_sum, f_sum):
            return jnp.sum(
                c_weight * (p * c_sum + cp_sum) + f_weight * f_sum, axis=0, keepdims=True
            )

        through_one = through(c_one, c_p, s_one)
        at = pl.ds(b, 1)
        for k in range(3):
            accel = KAPPA * (
                6.0 * (p * xm[k] + x[k] * m1 - s_m[5 + k : 6 + k])
                + 0.5 * (weighted[5 + k : 6 + k] - v[k] * w_u)
            )
            if k == 2:
                accel = accel - GRAVITY
            new_v = v[k] + DT * accel
            v_out[k, at] = new_v
            x_out[k, at] = x[k] + DT * new_v
            gv_out[k, at] = g[k] * (1.0 / DT) - (0.5 * KAPPA) * (g[k] * w_u - u * w_g[k])
            direct = 6.0 * (g[k] * (p * m0 + m1) - mass * (p * g0[k] + g1[k]))
            out[b, k : k + 1] = cot_x[k, at] + KAPPA * (
                direct - x[k] * through_one + through(c_x[k], c_px[k], s_x[k])
            )
            out[b, 3 + k : 4 + k] = xm[k]
        out[b, 6:7] = grad_m
        h_out[b] = (rho[b] * q) * (
            0.5 * (1.0 + 2.0 * q * q * q) * grad_p - q * q * grad_q
        )

    for_blocks(blocks, finish, unroll=2)


def run_force(entries, count, a, b, q, rho, cot_x):
    blocks = rho.shape[0]
    smem = pl.BlockSpec(memory_space=pltpu.SMEM)
    vmem = pl.BlockSpec(memory_space=pltpu.VMEM)
    plane = jax.ShapeDtypeStruct((3, blocks, 128), F32)
    return pl.pallas_call(
        force_kernel,
        out_shape=(
            plane,
            plane,
            plane,
            jax.ShapeDtypeStruct((blocks, 8, 128), F32),
            jax.ShapeDtypeStruct((blocks, 1, 128), F32),
        ),
        in_specs=[smem, smem] + [vmem] * 11,
        out_specs=(vmem,) * 5,
        scratch_shapes=[
            pltpu.VMEM((3 * blocks, 48, 128), BF16),
            pltpu.VMEM((blocks + 1, 48, 128), BF16),
            pltpu.VMEM((3 * blocks, 2 * F_ROWS, 128), BF16),
            pltpu.VMEM((3 * blocks, 2 * C_ROWS, 128), BF16),
            pltpu.VMEM((blocks + 1, F_ROWS + C_ROWS, 128), F32),
        ]
        + [
            pltpu.VMEM((LONG // 2, 128, 256), F32),
            pltpu.VMEM((LONG // 2, 256, 256), BF16),
            pltpu.VMEM((LONG // 2, 256, 256), BF16),
        ]
        * 2,
        compiler_params=pltpu.CompilerParams(vmem_limit_bytes=58 << 20),
        name="force",
    )(entries, count, *a, *b, *q, rho, cot_x)


def adjoint_kernel(
    entries, count, a_prev, a_own, a_next, h_prev, h_own, h_next, partial, occupied,
    gx_out, gm_out, sources, targets, channels, acc, *buffers,
):
    blocks = a_own.shape[0]
    parts = ((a_prev, h_prev), (a_own, h_own), (a_next, h_next))

    def prepare(b):
        for part, (a_ref, h_ref) in enumerate(parts):
            at = part * blocks + b
            a = a_ref[b]
            e = basis(a)
            sources[at] = source_features(e)
            channels[at] = stacked([h_ref[b] * e])
            if part == 1:
                targets[b] = target_features(target_basis(a))
                acc[b] = jnp.zeros((8, 128), F32)

    for_blocks(blocks, prepare, unroll=4)
    targets[blocks] = jnp.zeros((48, 128), BF16)
    acc[blocks] = jnp.zeros((8, 128), F32)

    def step(t, now, later):
        newest, oldest = group_at(entries, t, SHORT), group_at(entries, t - 2, SHORT)
        for k in range(SHORT // 2):
            add_both(
                acc, oldest[k], slice(0, 8), matrix_sum(channels[oldest[k][2]], now[1][k])
            )
            split_into(later[1:], now[0], k, (2,))
            make_tiles(sources, targets, newest[k], later[0], k)

    group_loop(count, SHORT, 3, (buffers[:2], buffers[2:]), step)

    def finish(b):
        a = a_own[b]
        s = acc[b]
        h = h_own[b]
        mass = a[5:6]
        grad_m = partial[b, 6:7] + KAPPA * jnp.sum(s * target_basis(a), axis=0, keepdims=True)
        at = pl.ds(b, 1)
        gm_out[at] = grad_m * occupied[at]
        for k in range(3):
            pull = h * partial[b, 3 + k : 4 + k] + mass * (
                a[2 + k : 3 + k] * s[0:1] - s[2 + k : 3 + k]
            )
            gx_out[k, at] = partial[b, k : k + 1] - (6.0 * KAPPA) * pull

    for_blocks(blocks, finish, unroll=4)


def run_adjoint(entries, count, a, h, partial, occupied):
    blocks = partial.shape[0]
    smem = pl.BlockSpec(memory_space=pltpu.SMEM)
    vmem = pl.BlockSpec(memory_space=pltpu.VMEM)
    return pl.pallas_call(
        adjoint_kernel,
        out_shape=(
            jax.ShapeDtypeStruct((3, blocks, 128), F32),
            jax.ShapeDtypeStruct((blocks, 128), F32),
        ),
        in_specs=[smem, smem] + [vmem] * 8,
        out_specs=(vmem, vmem),
        scratch_shapes=[
            pltpu.VMEM((3 * blocks, 48, 128), BF16),
            pltpu.VMEM((blocks + 1, 48, 128), BF16),
            pltpu.VMEM((3 * blocks, 16, 128), BF16),
            pltpu.VMEM((blocks + 1, 8, 128), F32),
        ]
        + [
            pltpu.VMEM((SHORT // 2, 128, 256), F32),
            pltpu.VMEM((SHORT // 2, 256, 256), BF16),
        ]
        * 2,
        compiler_params=pltpu.CompilerParams(vmem_limit_bytes=58 << 20),
        name="adjoint",
    )(entries, count, *a, *h, partial, occupied)


def exchange_kernel(arrays, *refs):
    mine, previous, following = refs[:arrays], refs[arrays : 2 * arrays], refs[2 * arrays : 3 * arrays]
    send, receive = refs[3 * arrays :]
    devices = lax.axis_size("slab")
    me = lax.axis_index("slab")
    right, left = lax.rem(me + 1, devices), lax.rem(me + devices - 1, devices)
    mesh_id = pl.DeviceIdType.MESH
    barrier = pltpu.get_barrier_semaphore()
    for neighbour in (left, right):
        pl.semaphore_signal(barrier, inc=1, device_id=(neighbour,), device_id_type=mesh_id)
    pl.semaphore_wait(barrier, 2)
    copies = []
    for k in range(arrays):
        for way, (target, landing) in enumerate(((right, previous[k]), (left, following[k]))):
            copies.append(
                pltpu.make_async_remote_copy(
                    src_ref=mine[k],
                    dst_ref=landing,
                    send_sem=send.at[2 * k + way],
                    recv_sem=receive.at[2 * k + way],
                    device_id=(target,),
                    device_id_type=mesh_id,
                )
            )
            copies[-1].start()
    for copy in copies:
        copy.wait()


def exchange(identity, *values):
    count = len(values)
    anywhere = pl.BlockSpec(memory_space=pl.ANY)
    shapes = tuple(jax.ShapeDtypeStruct(v.shape, v.dtype) for v in values)
    got = pl.pallas_call(
        functools.partial(exchange_kernel, count),
        out_shape=shapes * 2,
        in_specs=[anywhere] * count,
        out_specs=(anywhere,) * (2 * count),
        scratch_shapes=[
            pltpu.SemaphoreType.DMA((2 * count,)),
            pltpu.SemaphoreType.DMA((2 * count,)),
        ],
        compiler_params=pltpu.CompilerParams(collective_id=identity, has_side_effects=True),
        name=f"exchange_{identity}",
    )(*values)
    return [(got[k], values[k], got[count + k]) for k in range(count)]


def cube_root(mass):
    safe = jnp.where(mass > 0.0, mass, 1.0)
    root = jnp.exp(jnp.log(safe) * (1.0 / 3.0))
    root = root - (root * root * root - safe) / (3.0 * root * root)
    return jnp.where(mass > 0.0, root, 0.0)


def local(positions, velocity, masses, counts, pair_home, pair_far, pair_owner, cot_x, cot_v):
    occupied = (lax.broadcasted_iota(jnp.int32, masses.shape, 1) < counts[:, None]).astype(F32)
    mass = (masses * occupied)[:, None, :]
    g = DT * (cot_v + DT * cot_x)

    def product(first, second):
        return jnp.sum(first * second, axis=1, keepdims=True)

    one = jnp.ones_like(mass)
    a_own = jnp.concatenate(
        [
            one, product(positions, positions), positions, mass, cube_root(mass),
            product(positions, g),
        ],
        axis=1,
    )
    b_own = jnp.concatenate([g, product(velocity, g), one, velocity], axis=1)
    mine, size, theirs = tile_lists(pair_home, pair_far, pair_owner)
    a, b, lists = exchange(0, a_own, b_own, theirs)
    entries, count = whole_list(mine, size, lists[0])
    pq, rho = run_density(entries, count, *a)
    (q,) = exchange(1, pq)
    planes = jnp.transpose(cot_x, (1, 0, 2))
    new_x, new_v, grad_v, partial, h = run_force(entries, count, a, b, q, rho, planes)
    (h_all,) = exchange(2, h)
    grad_x, grad_m = run_adjoint(entries, count, a, h_all, partial, occupied)

    def blocks_first(value):
        return jnp.transpose(value, (1, 0, 2))

    return (
        blocks_first(new_x), blocks_first(new_v), blocks_first(grad_x), blocks_first(grad_v),
        grad_m,
    )


def solution(mesh):
    block = P("slab", None, None)
    flat = P("slab")
    return jax.shard_map(
        local,
        mesh=mesh,
        in_specs=(block, block, P("slab", None), flat, flat, flat, flat, block, block),
        out_specs=(block, block, block, block, P("slab", None)),
        check_vma=False,
    )
```

time: 240 us -> 218 us (0.908)
  the two profiles are of different devices: /device:TPU:6 before, /device:TPU:127 now
where the time goes in v2:
time: 218 us
  Pallas kernels  196 us (90%)
  other arithmetic  13.8 us (6%)
  local copies, waits for them, and re-layouts  5.01 us (2%)
  between operations  3.39 us (2%)
    pallas_call x1, Pallas kernels, run_force(): pl.pallas_call(force_kernel, out_shape=(plane, plane, plane, jax.ShapeDty...  80.3 us
    pallas_call x1, Pallas kernels, run_adjoint(): pl.pallas_call(adjoint_kernel, out_shape=(jax.ShapeDtypeStruct((3, blocks...  42.3 us
    pallas_call x3, Pallas kernels, exchange(): pl.pallas_call(functools.partial(exchange_kernel, count), out_shape=shape...  39.9 us
    pallas_call x1, Pallas kernels, run_density(): pl.pallas_call(density_kernel, out_shape=(jax.ShapeDtypeStruct((blocks, 2...  33.3 us

profile of v2, /device:TPU:127, one launch (start us, length us, event | category | flops | bytes accessed | tf_op | source)
XLA Modules:
  0.0 218.0 jit_solution(1849639529896351184)
XLA Ops:
  0.6 0.7 multiply_add_fusion.1
  1.4 2.1 fusion
  3.5 1.4 fusion.11
  4.8 1.3 convert_reduce_fusion
  6.1 0.7 broadcast_subtract_fusion
  6.8 1.1 select_reduce_fusion.2
  8.0 0.7 pad.2.clone
  8.7 0.7 add_add_fusion.refs_2_
  9.4 2.1 multiply_reduce_fusion
  11.5 0.0 copy-start.2
  11.5 0.0 copy-start.3
  11.5 0.0 copy-start
  11.6 1.1 pad_maximum_fusion.refs_1_.b_own
  12.6 0.0 copy-done.2
  12.6 0.0 copy-done.3
  12.6 0.1 compare_select_fusion
  12.7 0.0 copy-done
  12.8 1.5 concatenate.37.refs_0_.a_own
  14.3 20.2 %exchange_0.1 = (f32[128,8,128]{2,1,0:T(8,128)}, f32[128,8,128]{2,1,0:T(8,128)}, s32[3,768]{1,0:T(4,128)}, f32[128,8,128]{2,1,0:T(8,128)}, f32[128,8,128]{2,1,0:T(8,128)}, /*index=5*/s32[3,768]{1,0:T(4,128)}) custom-call(f32[128,8,128]{2,1,0:T(8,128)} %concatenate.37.refs_0_.a_own, f32[128,8,128]{2,1,0:T(8,128)} %pad_maximum_fusion.refs_1_.b_own, ...), custom_call_target="tpu_custom_call" | custom-call | tf_op jit(solution)/shard_map/exchange_0/pallas_call | solution.py:553
  34.5 1.2 slice.15
  37.0 0.6 broadcast_in_dim.97.count
  37.5 0.8 add_reduce_fusion.2
  38.3 1.0 select_reduce_fusion
  39.4 0.1 concatenate.36
  40.8 0.3 dynamic_update_slice.3.entries
  41.1 0.0 copy-start.1
  41.1 0.6 copy-done.1
  41.7 33.3 %density.1 = (f32[128,2,128]{2,1,0:T(2,128)}, f32[128,1,128]{2,1,0:T(1,128)}) custom-call(s32[2624]{0:T(1024)} %copy-done.1, s32[8]{0:T(128)} %broadcast_in_dim.97.count, f32[128,8,128]{2,1,0:T(8,128)} %get-tuple-element.24.a_prev, f32[128,8,128]{2,1,0:T(8,128)} %concatenate.37.refs_0_.a_own, f32[128,8,128]{2,1,0:T(8,128)} %get-tuple-element.25.a_next), custom_call_target="tpu_custom_call" | custom-call | tf_op jit(solution)/shard_map/density/pallas_call | solution.py:212
  75.0 10.2 %exchange_1.1 = (f32[128,2,128]{2,1,0:T(2,128)}, f32[128,2,128]{2,1,0:T(2,128)}) custom-call(f32[128,2,128]{2,1,0:T(2,128)} %get-tuple-element.28.refs_0_.q_own), custom_call_target="tpu_custom_call" | custom-call | tf_op jit(solution)/shard_map/exchange_1/pallas_call | solution.py:553
  85.2 80.3 %force.1 = (f32[3,128,128]{2,1,0:T(8,128)}, f32[3,128,128]{2,1,0:T(8,128)}, f32[3,128,128]{2,1,0:T(8,128)}, f32[128,8,128]{2,1,0:T(8,128)}, f32[128,1,128]{2,1,0:T(1,128)}) custom-call(s32[2624]{0:T(1024)} %copy-done.1, s32[8]{0:T(128)} %broadcast_in_dim.97.count, f32[128,8,128]{2,1,0:T(8,128)} %get-tuple-element.24.a_prev, ...), custom_call_target="tpu_custom_call" | custom-call | tf_op jit(solution)/shard_map/force/pallas_call | solution.py:413
  165.5 9.5 %exchange_2.1 = (f32[128,1,128]{2,1,0:T(1,128)}, f32[128,1,128]{2,1,0:T(1,128)}) custom-call(f32[128,1,128]{2,1,0:T(1,128)} %get-tuple-element.34.refs_0_.h_own), custom_call_target="tpu_custom_call" | custom-call | tf_op jit(solution)/shard_map/exchange_2/pallas_call | solution.py:553
  174.9 0.7 fusion.6.occupied
  175.6 42.3 %adjoint.1 = (f32[3,128,128]{2,1,0:T(8,128)}, f32[128,128]{1,0:T(8,128)}) custom-call(s32[2624]{0:T(1024)} %copy-done.1, s32[8]{0:T(128)} %broadcast_in_dim.97.count, f32[128,8,128]{2,1,0:T(8,128)} %get-tuple-element.24.a_prev, f32[128,8,128]{2,1,0:T(8,128)} %concatenate.37.refs_0_.a_own, f32[128,8,128]{2,1,0:T(8,128)} %get-tuple-element.25.a_next, ...), custom_call_target="tpu_custom_call" | custom-call | tf_op jit(solution)/shard_map/adjoint/pallas_call | solution.py:496
  (11 shorter events, 0.1 us)
Async XLA Ops:
  11.5 1.1 copy-start.2
  11.5 1.1 copy-start.3
  11.5 1.2 copy-start
  41.1 0.6 copy-start.1

commit v3 on v2

--- a/solution.py
+++ b/solution.py
@@ -11,6 +11,7 @@
 GRAVITY = 1.0
 KAPPA = 1.0 / 128.0
 LEAD = 64
+DENSE = 64
 SHORT = 32
 LONG = 32
 F32 = jnp.float32
@@ -105,12 +106,32 @@
     return mine, size, theirs
 
 
-def whole_list(mine, size, previous):
-    codes = previous[0] * 512 + previous[1]
-    tail = jnp.full((codes.shape[0] + 2 * LEAD,), DEAD, jnp.int32)
-    entries = jnp.concatenate([tail[:LEAD], mine, tail])
-    entries = lax.dynamic_update_slice(entries, codes, (LEAD + size,))
-    return entries, jnp.broadcast_to(size + previous[2, 0], (8,))
+def merge_lists(mine, sizes, previous, entries, count):
+    size = sizes[0]
+    theirs = previous[2, 0] * sizes[1]
+
+    def chunks(length):
+        return lax.shift_right_logical(length + 15, 4)
+
+    for k in range(LEAD):
+        entries[k] = DEAD
+
+    def copy_mine(c, carry):
+        for k in range(16):
+            entries[LEAD + 16 * c + k] = mine[16 * c + k]
+        return carry
+
+    def copy_theirs(c, carry):
+        for k in range(16):
+            at = 16 * c + k
+            entries[LEAD + size + at] = previous[0, at] * 512 + previous[1, at]
+        return carry
+
+    lax.fori_loop(0, chunks(size), copy_mine, 0)
+    lax.fori_loop(0, chunks(theirs), copy_theirs, 0)
+    for k in range(2 * LEAD):
+        entries[LEAD + size + theirs + k] = DEAD
+    count[0] = size + theirs
 
 
 def group_at(entries, t, size):
@@ -135,7 +156,7 @@
     def body(half, carry):
         step(2 * half, even, odd)
 
-        @pl.when(groups > 0)
+        @pl.when(2 * half + 1 < groups + (stages - 1))
         def _():
             step(2 * half + 1, odd, even)
 
@@ -164,9 +185,11 @@
 
 
 def density_kernel(
-    entries, count, a_prev, a_own, a_next, out, rho_out, sources, targets, acc, *distances,
+    mine, sizes, previous, a_prev, a_own, a_next, out, rho_out, entries, count,
+    sources, targets, acc, *distances,
 ):
     blocks = a_own.shape[0]
+    merge_lists(mine, sizes, previous, entries, count)
 
     def prepare(b):
         for part, a_ref in enumerate((a_prev, a_own, a_next)):
@@ -181,15 +204,15 @@
     acc[blocks] = jnp.zeros((8, 128), F32)
 
     def step(t, now, later):
-        newer, older = group_at(entries, t, SHORT), group_at(entries, t - 1, SHORT)
-        for k in range(SHORT // 2):
+        newer, older = group_at(entries, t, DENSE), group_at(entries, t - 1, DENSE)
+        for k in range(DENSE // 2):
             c = now[k]
             mass_kernel = c * c * c
             total = jnp.sum(mass_kernel.reshape(16, 8, 256), axis=0)
             add_both(acc, older[k], slice(0, 8), total)
             make_tiles(sources, targets, newer[k], later, k)
 
-    group_loop(count, SHORT, 2, distances, step)
+    group_loop(count, DENSE, 2, distances, step)
 
     def finish(b):
         density = KAPPA * jnp.sum(acc[b], axis=0, keepdims=True)
@@ -205,7 +228,7 @@
     for_blocks(blocks, finish, unroll=8)
 
 
-def run_density(entries, count, a_prev, a_own, a_next):
+def run_density(mine, sizes, previous, a_prev, a_own, a_next):
     blocks = a_own.shape[0]
     smem = pl.BlockSpec(memory_space=pltpu.SMEM)
     vmem = pl.BlockSpec(memory_space=pltpu.VMEM)
@@ -214,18 +237,20 @@
         out_shape=(
             jax.ShapeDtypeStruct((blocks, 2, 128), F32),
             jax.ShapeDtypeStruct((blocks, 1, 128), F32),
+            jax.ShapeDtypeStruct((mine.shape[0] + previous.shape[1] + 3 * LEAD,), jnp.int32),
+            jax.ShapeDtypeStruct((8,), jnp.int32),
         ),
-        in_specs=[smem, smem, vmem, vmem, vmem],
-        out_specs=(vmem, vmem),
+        in_specs=[smem, smem, smem, vmem, vmem, vmem],
+        out_specs=(vmem, vmem, smem, smem),
         scratch_shapes=[
             pltpu.VMEM((3 * blocks, 48, 128), BF16),
             pltpu.VMEM((blocks + 1, 48, 128), BF16),
             pltpu.VMEM((blocks + 1, 8, 128), F32),
         ]
-        + [pltpu.VMEM((SHORT // 2, 128, 256), F32)] * 2,
+        + [pltpu.VMEM((DENSE // 2, 128, 256), F32)] * 2,
         compiler_params=pltpu.CompilerParams(vmem_limit_bytes=58 << 20),
         name="density",
-    )(entries, count, a_prev, a_own, a_next)
+    )(mine, sizes, previous, a_prev, a_own, a_next)
 
 
 F_ROWS = 56
@@ -522,28 +547,56 @@
     send, receive = refs[3 * arrays :]
     devices = lax.axis_size("slab")
     me = lax.axis_index("slab")
-    right, left = lax.rem(me + 1, devices), lax.rem(me + devices - 1, devices)
     mesh_id = pl.DeviceIdType.MESH
     barrier = pltpu.get_barrier_semaphore()
-    for neighbour in (left, right):
-        pl.semaphore_signal(barrier, inc=1, device_id=(neighbour,), device_id_type=mesh_id)
-    pl.semaphore_wait(barrier, 2)
-    copies = []
-    for k in range(arrays):
-        for way, (target, landing) in enumerate(((right, previous[k]), (left, following[k]))):
-            copies.append(
-                pltpu.make_async_remote_copy(
-                    src_ref=mine[k],
-                    dst_ref=landing,
-                    send_sem=send.at[2 * k + way],
-                    recv_sem=receive.at[2 * k + way],
-                    device_id=(target,),
-                    device_id_type=mesh_id,
-                )
-            )
-            copies[-1].start()
-    for copy in copies:
-        copy.wait()
+    has_left, has_right = me > 0, me < devices - 1
+    left, right = lax.rem(me + devices - 1, devices), lax.rem(me + 1, devices)
+
+    def copies(way):
+        target, landing = ((right, previous), (left, following))[way]
+        return [
+            pltpu.make_async_remote_copy(
+                src_ref=mine[k],
+                dst_ref=landing[k],
+                send_sem=send.at[2 * k + way],
+                recv_sem=receive.at[2 * k + way],
+                device_id=(target,),
+                device_id_type=mesh_id,
+            )
+            for k in range(arrays)
+        ]
+
+    for there, neighbour in ((has_left, left), (has_right, right)):
+
+        @pl.when(there)
+        def _(neighbour=neighbour):
+            pl.semaphore_signal(barrier, inc=1, device_id=(neighbour,), device_id_type=mesh_id)
+
+    at_end = jnp.logical_or(me == 0, me == devices - 1)
+
+    @pl.when(at_end)
+    def _():
+        pl.semaphore_wait(barrier, 1)
+
+    @pl.when(jnp.logical_not(at_end))
+    def _():
+        pl.semaphore_wait(barrier, 2)
+
+    for there, way in ((has_right, 0), (has_left, 1)):
+
+        @pl.when(there)
+        def _(way=way):
+            for copy in copies(way):
+                copy.start()
+
+    for there, way in ((has_right, 0), (has_left, 1)):
+
+        @pl.when(there)
+        def _(way=way):
+            for copy in copies(way):
+                copy.wait_send()
+            for copy in copies(1 - way):
+                copy.wait_recv()
 
 
 def exchange(identity, *values):
@@ -591,8 +644,9 @@
     b_own = jnp.concatenate([g, product(velocity, g), one, velocity], axis=1)
     mine, size, theirs = tile_lists(pair_home, pair_far, pair_owner)
     a, b, lists = exchange(0, a_own, b_own, theirs)
-    entries, count = whole_list(mine, size, lists[0])
-    pq, rho = run_density(entries, count, *a)
+    has_previous = (lax.axis_index("slab") > 0).astype(jnp.int32)
+    sizes = jnp.stack([size, has_previous])
+    pq, rho, entries, count = run_density(mine, sizes, lists[0], *a)
     (q,) = exchange(1, pq)
     planes = jnp.transpose(cot_x, (1, 0, 2))
     new_x, new_v, grad_v, partial, h = run_force(entries, count, a, b, q, rho, planes)

time: 218 us -> 192 us (0.88)
  the two profiles are of different devices: /device:TPU:127 before, /device:TPU:6 now
where the time goes in v3:
time: 192 us
  Pallas kernels  174 us (91%)
  other arithmetic  14.8 us (8%)
  local copies, waits for them, and re-layouts  2.09 us (1%)
    pallas_call x1, Pallas kernels, run_force(): pl.pallas_call(force_kernel, out_shape=(plane, plane, plane, jax.ShapeDty...  70.4 us
    pallas_call x3, Pallas kernels, exchange(): pl.pallas_call(functools.partial(exchange_kernel, count), out_shape=shape...  37.2 us
    pallas_call x1, Pallas kernels, run_adjoint(): pl.pallas_call(adjoint_kernel, out_shape=(jax.ShapeDtypeStruct((3, blocks...  36.8 us
    pallas_call x1, Pallas kernels, run_density(): pl.pallas_call(density_kernel, out_shape=(jax.ShapeDtypeStruct((blocks, 2...  29.5 us

profile of v3, /device:TPU:6, one launch (start us, length us, event | category | flops | bytes accessed | tf_op | source)
XLA Modules:
  0.0 191.6 jit_solution(16789768763087141799)
XLA Ops:
  0.6 0.7 multiply_add_fusion.1
  1.4 2.1 %fusion = (s32[1408]{0:T(1024)S(1)}, s32[1408]{0:T(1024)S(1)}, s32[1408]{0:T(1024)S(1)}) fusion(s32[1408]{0:T(1024)S(1)} %get-tuple-element.55), kind=kLoop, calls=%fused_computation.6 | loop fusion | flops 19820416 | bytes 22528 | tf_op jit(solution)/shard_map/reduce_sum | solution.py:82
  3.5 1.4 fusion.11
  4.8 1.3 convert_reduce_fusion
  6.1 0.7 broadcast_subtract_fusion
  6.8 1.1 select_reduce_fusion.2
  8.0 0.7 pad.2.clone
  8.7 0.7 add_add_fusion.refs_2_
  9.4 2.1 %multiply_reduce_fusion = (f32[128,128]{1,0:T(8,128)S(1)}, f32[128,128]{1,0:T(8,128)S(1)}, f32[128,3,128]{2,1,0:T(4,128)S(1)}, f32[128,3,128]{2,1,0:T(4,128)S(1)}, f32[128,3,128]{2,1,0:T(4,128)S(1)}) fusion(f32[128,3,128]{2,0,1:T(8,128)} %param.10, f32[128,3,128]{2,0,1:T(8,128)} %param.9, f32[128,3,128]{2,0,1:T(8,128)} %param.16, f32[128,3,128]{2,0,1:T(8,128)} %param.17), kind=kLoop, calls=%fused_computation.18 | loop fusion | flops 311296 | bytes 1507328 | tf_op jit(solution)/shard_map/reduce_sum | solution.py:634
  11.5 0.0 copy-start.1
  11.5 0.0 copy-start.2
  11.5 0.0 copy-start
  11.6 1.1 pad_maximum_fusion.refs_1_.b_own
  12.6 0.0 copy-done.1
  12.6 0.0 copy-done.2
  12.6 0.1 compare_select_fusion
  12.7 0.0 copy-done
  12.8 1.3 concatenate.33.refs_0_.a_own
  14.1 19.9 %exchange_0.1 = (f32[128,8,128]{2,1,0:T(8,128)}, f32[128,8,128]{2,1,0:T(8,128)}, s32[3,768]{1,0:T(4,128)}, f32[128,8,128]{2,1,0:T(8,128)}, f32[128,8,128]{2,1,0:T(8,128)}, /*index=5*/s32[3,768]{1,0:T(4,128)}) custom-call(f32[128,8,128]{2,1,0:T(8,128)} %concatenate.33.refs_0_.a_own, f32[128,8,128]{2,1,0:T(8,128)} %pad_maximum_fusion.refs_1_.b_own, ...), custom_call_target="tpu_custom_call" | custom-call | tf_op jit(solution)/shard_map/exchange_0/pallas_call | solution.py:606
  34.0 1.0 select_reduce_fusion
  35.0 0.6 broadcast_add_fusion.1.mine
  35.6 1.2 pad_add_fusion.2.sizes
  36.8 29.5 %density.1 = (f32[128,2,128]{2,1,0:T(2,128)}, f32[128,1,128]{2,1,0:T(1,128)}, s32[2624]{0:T(1024)}, s32[8]{0:T(128)}) custom-call(s32[1664]{0:T(1024)} %broadcast_add_fusion.1.mine, s32[2]{0:T(128)} %pad_add_fusion.2.sizes, s32[3,768]{1,0:T(4,128)} %get-tuple-element.25.previous, f32[128,8,128]{2,1,0:T(8,128)} %get-tuple-element.26.a_prev, ...), custom_call_target="tpu_custom_call" | custom-call | tf_op jit(solution)/shard_map/density/pallas_call | solution.py:235
  66.3 9.0 %exchange_1.1 = (f32[128,2,128]{2,1,0:T(2,128)}, f32[128,2,128]{2,1,0:T(2,128)}) custom-call(f32[128,2,128]{2,1,0:T(2,128)} %get-tuple-element.32.refs_0_.q_own), custom_call_target="tpu_custom_call" | custom-call | tf_op jit(solution)/shard_map/exchange_1/pallas_call | solution.py:606
  75.4 70.4 %force.1 = (f32[3,128,128]{2,1,0:T(8,128)}, f32[3,128,128]{2,1,0:T(8,128)}, f32[3,128,128]{2,1,0:T(8,128)}, f32[128,8,128]{2,1,0:T(8,128)}, f32[128,1,128]{2,1,0:T(1,128)}) custom-call(s32[2624]{0:T(1024)} %get-tuple-element.28.entries, s32[8]{0:T(128)} %get-tuple-element.29.count, f32[128,8,128]{2,1,0:T(8,128)} %get-tuple-element.26.a_prev, ...), custom_call_target="tpu_custom_call" | custom-call | tf_op jit(solution)/shard_map/force/pallas_call | solution.py:438
  145.8 8.3 %exchange_2.1 = (f32[128,1,128]{2,1,0:T(1,128)}, f32[128,1,128]{2,1,0:T(1,128)}) custom-call(f32[128,1,128]{2,1,0:T(1,128)} %get-tuple-element.38.refs_0_.h_own), custom_call_target="tpu_custom_call" | custom-call | tf_op jit(solution)/shard_map/exchange_2/pallas_call | solution.py:606
  154.1 0.7 fusion.6.occupied
  154.8 36.8 %adjoint.1 = (f32[3,128,128]{2,1,0:T(8,128)}, f32[128,128]{1,0:T(8,128)}) custom-call(s32[2624]{0:T(1024)} %get-tuple-element.28.entries, s32[8]{0:T(128)} %get-tuple-element.29.count, f32[128,8,128]{2,1,0:T(8,128)} %get-tuple-element.26.a_prev, f32[128,8,128]{2,1,0:T(8,128)} %concatenate.33.refs_0_.a_own, f32[128,8,128]{2,1,0:T(8,128)} %get-tuple-element.27.a_next, ...), custom_call_target="tpu_custom_call" | custom-call | tf_op jit(solution)/shard_map/adjoint/pallas_call | solution.py:521
  (8 shorter events, 0.1 us)
Async XLA Ops:
  11.5 1.1 copy-start.1
  11.5 1.1 copy-start.2
  11.5 1.2 copy-start

commit v4 on v3

--- a/solution.py
+++ b/solution.py
@@ -10,9 +10,9 @@
 DT = 0.1
 GRAVITY = 1.0
 KAPPA = 1.0 / 128.0
-LEAD = 64
+LEAD = 128
 DENSE = 64
-SHORT = 32
+SHORT = 64
 LONG = 32
 F32 = jnp.float32
 BF16 = jnp.bfloat16
@@ -52,15 +52,34 @@
     return lax.broadcasted_iota(jnp.int32, (8, 128), 0)
 
 
-def basis(a):
-    return jnp.where(row_index() < 5, a, 0.0)
-
-
-def target_basis(a):
+def rows_at(ref, b):
+    return [ref[b, k : k + 1] for k in range(ref.shape[1])]
+
+
+def rows_of(values):
     row = row_index()
-    return jnp.where(
-        row == 0, 1.0 - a[1:2], jnp.where(row == 1, -1.0, jnp.where(row < 5, 2.0 * a, 0.0))
-    )
+    out = values[-1]
+    for k in reversed(range(len(values) - 1)):
+        out = jnp.where(row == k, values[k], out)
+    return jnp.broadcast_to(out, (8, 128))
+
+
+def inner(first, second):
+    return first[0] * second[0] + first[1] * second[1] + first[2] * second[2]
+
+
+def unpack(ref, b):
+    rows = rows_at(ref, b)
+    x, root = rows[:3], rows[3]
+    return x, inner(x, x), root, root * root * root
+
+
+def basis(x, norm):
+    return rows_of([1.0, norm] + x + [0.0])
+
+
+def target_basis(x, norm):
+    return rows_of([1.0 - norm, -1.0] + [2.0 * value for value in x] + [0.0])
 
 
 DEAD = 128 * 512 + 128
@@ -193,10 +212,10 @@
 
     def prepare(b):
         for part, a_ref in enumerate((a_prev, a_own, a_next)):
-            a = a_ref[b]
-            sources[part * blocks + b] = source_features(basis(a) * a[6:7])
+            x, norm, root, _ = unpack(a_ref, b)
+            sources[part * blocks + b] = source_features(basis(x, norm) * root)
             if part == 1:
-                targets[b] = target_features(target_basis(a))
+                targets[b] = target_features(target_basis(x, norm))
                 acc[b] = jnp.zeros((8, 128), F32)
 
     for_blocks(blocks, prepare, unroll=4)
@@ -280,52 +299,49 @@
     return both[:rows] + both[rows:]
 
 
-def pair_basis(a, p):
-    row = row_index()
-    e = basis(a)
-    return jnp.where(row >= 5, p * pltpu.roll(e, 3, 0), jnp.where(row == 1, p, e))
-
-
-def force_channels(a, b, p, q):
-    row = row_index()
-    x = [a[2 + k : 3 + k] for k in range(3)]
-    mass, xg = a[5:6], a[7:8]
-    first = jnp.where(row >= 4, (mass * q) * b, b)
-    with_p = jnp.where(row < 3, p * b, jnp.where(row == 3, p * xg, 0.0))
-    second = jnp.where(
-        row == 0,
-        mass,
-        jnp.where(
-            row < 4, mass * pltpu.roll(a, 7, 0), jnp.where(row < 7, pltpu.roll(b, 4, 0), xg)
-        ),
-    )
+def force_channels(x, norm, mass, v, g, p, q):
+    u = mass * q
+    xg = inner(x, g)
+    px = [p * value for value in x]
+    first = rows_of(g + [inner(v, g), u] + [u * value for value in v])
+    with_p = rows_of([p * value for value in g] + [p * xg, 0.0])
+    second = rows_of([mass] + [mass * value for value in x] + g + [xg])
     second_p = p * second
-    f = [first, a[1:2] * first] + [x[k] * first for k in range(3)]
-    f += [mass * pair_basis(a, p), with_p]
-    c = [second] + [x[k] * second for k in range(3)]
-    c += [second_p] + [x[k] * second_p for k in range(3)]
+    f = [first, norm * first] + [value * first for value in x]
+    f += [mass * rows_of([1.0, p] + x + px), with_p]
+    c = [second] + [value * second for value in x]
+    c += [second_p] + [value * second for value in px]
     return stacked(f), stacked(c)
 
 
+def velocity_rows(b_ref, g_ref, b):
+    rows, rest = rows_at(b_ref, b), rows_at(g_ref, b)
+    return rows[:3], [rows[3]] + rest
+
+
 def force_kernel(
-    entries, count, a_prev, a_own, a_next, b_prev, b_own, b_next, q_prev, q_own, q_next,
-    rho, cot_x, x_out, v_out, gv_out, out, h_out, sources, targets, f_channels, c_channels, acc,
+    entries, count, a_prev, a_own, a_next, b_prev, b_own, b_next, g_prev, g_own, g_next,
+    q_prev, q_own, q_next, rho, cot_x, x_out, v_out, gv_out, out, h_out, sources, targets, f_channels, c_channels, acc,
     *buffers,
 ):
     blocks = a_own.shape[0]
-    row = row_index()
-    parts = ((a_prev, b_prev, q_prev), (a_own, b_own, q_own), (a_next, b_next, q_next))
+    parts = (
+        (a_prev, b_prev, g_prev, q_prev),
+        (a_own, b_own, g_own, q_own),
+        (a_next, b_next, g_next, q_next),
+    )
 
     def prepare(b):
-        for part, (a_ref, b_ref, q_ref) in enumerate(parts):
+        for part, (a_ref, b_ref, g_ref, q_ref) in enumerate(parts):
             at = part * blocks + b
-            a = a_ref[b]
-            sources[at] = source_features(basis(a))
-            f, c = force_channels(a, b_ref[b], q_ref[b, 0:1], q_ref[b, 1:2])
+            x, norm, _, mass = unpack(a_ref, b)
+            v, g = velocity_rows(b_ref, g_ref, b)
+            sources[at] = source_features(basis(x, norm))
+            f, c = force_channels(x, norm, mass, v, g, q_ref[b, 0:1], q_ref[b, 1:2])
             f_channels[at] = f
             c_channels[at] = c
             if part == 1:
-                targets[b] = target_features(target_basis(a))
+                targets[b] = target_features(target_basis(x, norm))
                 acc[b] = jnp.zeros((F_ROWS + C_ROWS, 128), F32)
 
     for_blocks(blocks, prepare, unroll=2)
@@ -347,15 +363,10 @@
     group_loop(count, LONG, 3, (buffers[:3], buffers[3:]), step)
 
     def finish(b):
-        a = a_own[b]
-        bb = b_own[b]
+        x, n, _, mass = unpack(a_own, b)
+        v, g = velocity_rows(b_own, g_own, b)
         p, q = q_own[b, 0:1], q_own[b, 1:2]
-        n = a[1:2]
-        x = [a[2 + k : 3 + k] for k in range(3)]
-        g = [bb[k : k + 1] for k in range(3)]
-        v = [bb[5 + k : 6 + k] for k in range(3)]
-        vg = bb[3:4]
-        mass, xg = a[5:6], a[7:8]
+        vg, xg = inner(v, g), inner(x, g)
         u = mass * q
 
         def group(k):
@@ -384,19 +395,14 @@
         grad_m = KAPPA * (-6.0 * (p * xdg0 + xdg1) - 0.5 * q * energy)
         grad_q = (-0.5 * KAPPA) * mass * energy
         grad_p = (6.0 * KAPPA) * (g[0] * xm[0] + g[1] * xm[1] + g[2] * xm[2] - mass * xdg0)
-        c_weight = 24.0 * jnp.where(
-            row == 0,
-            xg,
-            jnp.where(
-                row < 4,
-                -pltpu.roll(bb, 1, 0),
-                jnp.where(row < 7, -mass * pltpu.roll(a, 2, 0), mass),
-            ),
+        mass24 = 24.0 * mass
+        c_weight = rows_of(
+            [24.0 * xg] + [-24.0 * value for value in g] + [-mass24 * value for value in x]
+            + [mass24]
         )
-        f_weight = 3.0 * jnp.where(
-            row < 3,
-            u * pltpu.roll(bb, 3, 0),
-            jnp.where(row == 3, -u, jnp.where(row == 4, -vg, pltpu.roll(bb, 5, 0))),
+        u3 = 3.0 * u
+        f_weight = rows_of(
+            [u3 * value for value in v] + [-u3, -3.0 * vg] + [3.0 * value for value in g]
         )
 
         def through(c_sum, cp_sum, f_sum):
@@ -430,7 +436,7 @@
     for_blocks(blocks, finish, unroll=2)
 
 
-def run_force(entries, count, a, b, q, rho, cot_x):
+def run_force(entries, count, a, b, g, q, rho, cot_x):
     blocks = rho.shape[0]
     smem = pl.BlockSpec(memory_space=pltpu.SMEM)
     vmem = pl.BlockSpec(memory_space=pltpu.VMEM)
@@ -444,7 +450,7 @@
             jax.ShapeDtypeStruct((blocks, 8, 128), F32),
             jax.ShapeDtypeStruct((blocks, 1, 128), F32),
         ),
-        in_specs=[smem, smem] + [vmem] * 11,
+        in_specs=[smem, smem] + [vmem] * 14,
         out_specs=(vmem,) * 5,
         scratch_shapes=[
             pltpu.VMEM((3 * blocks, 48, 128), BF16),
@@ -461,7 +467,7 @@
         * 2,
         compiler_params=pltpu.CompilerParams(vmem_limit_bytes=58 << 20),
         name="force",
-    )(entries, count, *a, *b, *q, rho, cot_x)
+    )(entries, count, *a, *b, *g, *q, rho, cot_x)
 
 
 def adjoint_kernel(
@@ -474,12 +480,12 @@
     def prepare(b):
         for part, (a_ref, h_ref) in enumerate(parts):
             at = part * blocks + b
-            a = a_ref[b]
-            e = basis(a)
+            x, norm, _, _ = unpack(a_ref, b)
+            e = basis(x, norm)
             sources[at] = source_features(e)
             channels[at] = stacked([h_ref[b] * e])
             if part == 1:
-                targets[b] = target_features(target_basis(a))
+                targets[b] = target_features(target_basis(x, norm))
                 acc[b] = jnp.zeros((8, 128), F32)
 
     for_blocks(blocks, prepare, unroll=4)
@@ -498,16 +504,17 @@
     group_loop(count, SHORT, 3, (buffers[:2], buffers[2:]), step)
 
     def finish(b):
-        a = a_own[b]
+        x, norm, _, mass = unpack(a_own, b)
         s = acc[b]
         h = h_own[b]
-        mass = a[5:6]
-        grad_m = partial[b, 6:7] + KAPPA * jnp.sum(s * target_basis(a), axis=0, keepdims=True)
+        grad_m = partial[b, 6:7] + KAPPA * jnp.sum(
+            s * target_basis(x, norm), axis=0, keepdims=True
+        )
         at = pl.ds(b, 1)
         gm_out[at] = grad_m * occupied[at]
         for k in range(3):
             pull = h * partial[b, 3 + k : 4 + k] + mass * (
-                a[2 + k : 3 + k] * s[0:1] - s[2 + k : 3 + k]
+                x[k] * s[0:1] - s[2 + k : 3 + k]
             )
             gx_out[k, at] = partial[b, k : k + 1] - (6.0 * KAPPA) * pull
 
@@ -630,26 +637,16 @@
     mass = (masses * occupied)[:, None, :]
     g = DT * (cot_v + DT * cot_x)
 
-    def product(first, second):
-        return jnp.sum(first * second, axis=1, keepdims=True)
-
-    one = jnp.ones_like(mass)
-    a_own = jnp.concatenate(
-        [
-            one, product(positions, positions), positions, mass, cube_root(mass),
-            product(positions, g),
-        ],
-        axis=1,
-    )
-    b_own = jnp.concatenate([g, product(velocity, g), one, velocity], axis=1)
+    a_own = jnp.concatenate([positions, cube_root(mass)], axis=1)
+    b_own = jnp.concatenate([velocity, g[:, 0:1]], axis=1)
     mine, size, theirs = tile_lists(pair_home, pair_far, pair_owner)
-    a, b, lists = exchange(0, a_own, b_own, theirs)
+    a, b, rest, lists = exchange(0, a_own, b_own, g[:, 1:3], theirs)
     has_previous = (lax.axis_index("slab") > 0).astype(jnp.int32)
     sizes = jnp.stack([size, has_previous])
     pq, rho, entries, count = run_density(mine, sizes, lists[0], *a)
     (q,) = exchange(1, pq)
     planes = jnp.transpose(cot_x, (1, 0, 2))
-    new_x, new_v, grad_v, partial, h = run_force(entries, count, a, b, q, rho, planes)
+    new_x, new_v, grad_v, partial, h = run_force(entries, count, a, b, rest, q, rho, planes)
     (h_all,) = exchange(2, h)
     grad_x, grad_m = run_adjoint(entries, count, a, h_all, partial, occupied)
 

time: 192 us -> 190 us (0.990)
    pallas_call x3, Pallas kernels: 37.2 us -> 33 us  [exchange(): pl.pallas_call(functools.partial(exchange_kernel, count), out_shape=shape...]
    pallas_call x1, Pallas kernels: 70.4 us -> 73.2 us  [run_force(): pl.pallas_call(force_kernel, out_shape=(plane, plane, plane, jax.ShapeDty...]
    reduce_sum x2 -> x0, other arithmetic: 2.13 us -> none  [product(): return jnp.sum(first * second, axis=1, keepdims=True)]
where the time goes in v4:
time: 190 us
  Pallas kernels  173 us (91%)
  other arithmetic  14.1 us (7%)
  local copies, waits for them, and re-layouts  2.25 us (1%)
    pallas_call x1, Pallas kernels, run_force(): pl.pallas_call(force_kernel, out_shape=(plane, plane, plane, jax.ShapeDty...  73.2 us
    pallas_call x1, Pallas kernels, run_adjoint(): pl.pallas_call(adjoint_kernel, out_shape=(jax.ShapeDtypeStruct((3, blocks...  36.7 us
    pallas_call x3, Pallas kernels, exchange(): pl.pallas_call(functools.partial(exchange_kernel, count), out_shape=shape...  33 us
    pallas_call x1, Pallas kernels, run_density(): pl.pallas_call(density_kernel, out_shape=(jax.ShapeDtypeStruct((blocks, 2...  29.9 us

profile of v4, /device:TPU:6, one launch (start us, length us, event | category | flops | bytes accessed | tf_op | source)
XLA Modules:
  0.0 189.8 jit_solution(17441029091988381874)
XLA Ops:
  0.6 0.7 multiply_add_fusion.1
  1.4 2.1 %fusion = (s32[1408]{0:T(1024)S(1)}, s32[1408]{0:T(1024)S(1)}, s32[1408]{0:T(1024)S(1)}) fusion(s32[1408]{0:T(1024)S(1)} %get-tuple-element.57), kind=kLoop, calls=%fused_computation.6 | loop fusion | flops 19820416 | bytes 22528 | tf_op jit(solution)/shard_map/reduce_sum | solution.py:101
  3.5 0.0 copy-start
  3.5 1.4 fusion.10
  4.9 1.3 convert_reduce_fusion
  6.2 0.7 broadcast_subtract_fusion
  6.8 1.1 select_reduce_fusion.2
  8.0 0.7 pad.2.clone
  8.7 0.7 add_add_fusion.refs_3_
  9.4 0.0 copy-start.1
  9.4 1.4 fusion.2
  10.8 0.0 copy-start.2
  10.8 0.0 copy-start.3
  10.9 0.0 copy-done
  10.9 0.1 copy.24
  11.0 0.0 copy-done.1
  11.0 0.1 copy.30
  11.2 0.5 copy-done.2
  11.6 0.0 copy-done.3
  11.6 0.1 compare_select_fusion
  11.8 1.0 pad_maximum_fusion
  12.8 0.7 slice.9.refs_2_.g_own
  13.5 15.7 %exchange_0.1 = (f32[128,4,128]{2,1,0:T(4,128)}, f32[128,4,128]{2,1,0:T(4,128)}, f32[128,2,128]{2,1,0:T(2,128)}, s32[3,768]{1,0:T(4,128)}, f32[128,4,128]{2,1,0:...) custom-call(f32[128,4,128]{2,1,0:T(4,128)} %get-tuple-element.70.refs_0_.a_own, ...), custom_call_target="tpu_custom_call" | custom-call | tf_op jit(solution)/shard_map/exchange_0/pallas_call | solution.py:613
  29.3 1.0 select_reduce_fusion
  30.3 0.6 broadcast_add_fusion.1.mine
  30.9 1.2 pad_add_fusion.2.sizes
  32.1 29.9 %density.1 = (f32[128,2,128]{2,1,0:T(2,128)}, f32[128,1,128]{2,1,0:T(1,128)}, s32[2816]{0:T(1024)}, s32[8]{0:T(128)}) custom-call(s32[1664]{0:T(1024)} %broadcast_add_fusion.1.mine, s32[2]{0:T(128)} %pad_add_fusion.2.sizes, s32[3,768]{1,0:T(4,128)} %get-tuple-element.27.previous, f32[128,4,128]{2,1,0:T(4,128)} %get-tuple-element.28.a_prev, ...), custom_call_target="tpu_custom_call" | custom-call | tf_op jit(solution)/shard_map/density/pallas_call | solution.py:254
  62.0 9.0 %exchange_1.1 = (f32[128,2,128]{2,1,0:T(2,128)}, f32[128,2,128]{2,1,0:T(2,128)}) custom-call(f32[128,2,128]{2,1,0:T(2,128)} %get-tuple-element.36.refs_0_.q_own), custom_call_target="tpu_custom_call" | custom-call | tf_op jit(solution)/shard_map/exchange_1/pallas_call | solution.py:613
  71.0 73.2 %force.1 = (f32[3,128,128]{2,1,0:T(8,128)}, f32[3,128,128]{2,1,0:T(8,128)}, f32[3,128,128]{2,1,0:T(8,128)}, f32[128,8,128]{2,1,0:T(8,128)}, f32[128,1,128]{2,1,0:T(1,128)}) custom-call(s32[2816]{0:T(1024)} %get-tuple-element.30.entries, s32[8]{0:T(128)} %get-tuple-element.31.count, f32[128,4,128]{2,1,0:T(4,128)} %get-tuple-element.28.a_prev, ...), custom_call_target="tpu_custom_call" | custom-call | tf_op jit(solution)/shard_map/force/pallas_call | solution.py:444
  144.2 8.3 %exchange_2.1 = (f32[128,1,128]{2,1,0:T(1,128)}, f32[128,1,128]{2,1,0:T(1,128)}) custom-call(f32[128,1,128]{2,1,0:T(1,128)} %get-tuple-element.42.refs_0_.h_own), custom_call_target="tpu_custom_call" | custom-call | tf_op jit(solution)/shard_map/exchange_2/pallas_call | solution.py:613
  152.5 0.7 fusion.6.occupied
  153.2 36.7 %adjoint.1 = (f32[3,128,128]{2,1,0:T(8,128)}, f32[128,128]{1,0:T(8,128)}) custom-call(s32[2816]{0:T(1024)} %get-tuple-element.30.entries, s32[8]{0:T(128)} %get-tuple-element.31.count, f32[128,4,128]{2,1,0:T(4,128)} %get-tuple-element.28.a_prev, f32[128,4,128]{2,1,0:T(4,128)} %get-tuple-element.70.refs_0_.a_own, f32[128,4,128]{2,1,0:T(4,128)} %get-tuple-element.29.a_next, ...), custom_call_target="tpu_custom_call" | custom-call | tf_op jit(solution)/shard_map/adjoint/pallas_call | solution.py:528
  (7 shorter events, 0.1 us)
Async XLA Ops:
  3.5 7.4 %copy-start = (f32[128,3,128]{2,0,1:T(8,128)S(1)}, f32[128,3,128]{2,0,1:T(8,128)}, u32[]{:S(2)}) copy-start(f32[128,3,128]{2,0,1:T(8,128)} %param.9) | copy-start | bytes 589828
  9.4 1.6 copy-start.1
  10.8 0.8 copy-start.2
  10.8 0.8 copy-start.3

commit v5 on v4

--- a/solution.py
+++ b/solution.py
@@ -11,7 +11,7 @@
 GRAVITY = 1.0
 KAPPA = 1.0 / 128.0
 LEAD = 128
-DENSE = 64
+DENSE = 128
 SHORT = 64
 LONG = 32
 F32 = jnp.float32

time: 190 us -> 188 us (0.989)
  Pallas kernels: 173 us -> 170 us
where the time goes in v5:
time: 188 us; the launch traced here: 187 us
  Pallas kernels  170 us (90%)
  other arithmetic  14.1 us (8%)
  local copies, waits for them, and re-layouts  2.25 us (1%)
    pallas_call x1, Pallas kernels, run_force(): pl.pallas_call(force_kernel, out_shape=(plane, plane, plane, jax.ShapeDty...  72.3 us
    pallas_call x1, Pallas kernels, run_adjoint(): pl.pallas_call(adjoint_kernel, out_shape=(jax.ShapeDtypeStruct((3, blocks...  35.6 us
    pallas_call x3, Pallas kernels, exchange(): pl.pallas_call(functools.partial(exchange_kernel, count), out_shape=shape...  33 us
    pallas_call x1, Pallas kernels, run_density(): pl.pallas_call(density_kernel, out_shape=(jax.ShapeDtypeStruct((blocks, 2...  28.6 us

profile of v5, /device:TPU:6, one launch (start us, length us, event | category | flops | bytes accessed | tf_op | source)
XLA Modules:
  0.0 186.6 jit_solution(8115458142266559368)
XLA Ops:
  0.6 0.7 multiply_add_fusion.1
  1.4 2.1 %fusion = (s32[1408]{0:T(1024)S(1)}, s32[1408]{0:T(1024)S(1)}, s32[1408]{0:T(1024)S(1)}) fusion(s32[1408]{0:T(1024)S(1)} %get-tuple-element.57), kind=kLoop, calls=%fused_computation.6 | loop fusion | flops 19820416 | bytes 22528 | tf_op jit(solution)/shard_map/reduce_sum | solution.py:101
  3.5 0.0 copy-start
  3.5 1.4 fusion.10
  4.9 1.3 convert_reduce_fusion
  6.2 0.7 broadcast_subtract_fusion
  6.8 1.1 select_reduce_fusion.2
  8.0 0.7 pad.2.clone
  8.7 0.7 add_add_fusion.refs_3_
  9.4 0.0 copy-start.1
  9.4 1.4 fusion.2
  10.8 0.0 copy-start.2
  10.8 0.0 copy-start.3
  10.9 0.0 copy-done
  10.9 0.1 copy.24
  11.0 0.0 copy-done.1
  11.0 0.1 copy.30
  11.2 0.5 copy-done.2
  11.6 0.0 copy-done.3
  11.6 0.1 compare_select_fusion
  11.8 1.0 pad_maximum_fusion
  12.8 0.7 slice.9.refs_2_.g_own
  13.5 15.7 %exchange_0.1 = (f32[128,4,128]{2,1,0:T(4,128)}, f32[128,4,128]{2,1,0:T(4,128)}, f32[128,2,128]{2,1,0:T(2,128)}, s32[3,768]{1,0:T(4,128)}, f32[128,4,128]{2,1,0:...) custom-call(f32[128,4,128]{2,1,0:T(4,128)} %get-tuple-element.70.refs_0_.a_own, ...), custom_call_target="tpu_custom_call" | custom-call | tf_op jit(solution)/shard_map/exchange_0/pallas_call | solution.py:613
  29.3 1.0 select_reduce_fusion
  30.3 0.6 broadcast_add_fusion.1.mine
  30.9 1.2 pad_add_fusion.2.sizes
  32.1 28.6 %density.1 = (f32[128,2,128]{2,1,0:T(2,128)}, f32[128,1,128]{2,1,0:T(1,128)}, s32[2816]{0:T(1024)}, s32[8]{0:T(128)}) custom-call(s32[1664]{0:T(1024)} %broadcast_add_fusion.1.mine, s32[2]{0:T(128)} %pad_add_fusion.2.sizes, s32[3,768]{1,0:T(4,128)} %get-tuple-element.27.previous, f32[128,4,128]{2,1,0:T(4,128)} %get-tuple-element.28.a_prev, ...), custom_call_target="tpu_custom_call" | custom-call | tf_op jit(solution)/shard_map/density/pallas_call | solution.py:254
  60.7 9.0 %exchange_1.1 = (f32[128,2,128]{2,1,0:T(2,128)}, f32[128,2,128]{2,1,0:T(2,128)}) custom-call(f32[128,2,128]{2,1,0:T(2,128)} %get-tuple-element.36.refs_0_.q_own), custom_call_target="tpu_custom_call" | custom-call | tf_op jit(solution)/shard_map/exchange_1/pallas_call | solution.py:613
  69.7 72.3 %force.1 = (f32[3,128,128]{2,1,0:T(8,128)}, f32[3,128,128]{2,1,0:T(8,128)}, f32[3,128,128]{2,1,0:T(8,128)}, f32[128,8,128]{2,1,0:T(8,128)}, f32[128,1,128]{2,1,0:T(1,128)}) custom-call(s32[2816]{0:T(1024)} %get-tuple-element.30.entries, s32[8]{0:T(128)} %get-tuple-element.31.count, f32[128,4,128]{2,1,0:T(4,128)} %get-tuple-element.28.a_prev, ...), custom_call_target="tpu_custom_call" | custom-call | tf_op jit(solution)/shard_map/force/pallas_call | solution.py:444
  142.0 8.3 %exchange_2.1 = (f32[128,1,128]{2,1,0:T(1,128)}, f32[128,1,128]{2,1,0:T(1,128)}) custom-call(f32[128,1,128]{2,1,0:T(1,128)} %get-tuple-element.42.refs_0_.h_own), custom_call_target="tpu_custom_call" | custom-call | tf_op jit(solution)/shard_map/exchange_2/pallas_call | solution.py:613
  150.3 0.7 fusion.6.occupied
  151.0 35.6 %adjoint.1 = (f32[3,128,128]{2,1,0:T(8,128)}, f32[128,128]{1,0:T(8,128)}) custom-call(s32[2816]{0:T(1024)} %get-tuple-element.30.entries, s32[8]{0:T(128)} %get-tuple-element.31.count, f32[128,4,128]{2,1,0:T(4,128)} %get-tuple-element.28.a_prev, f32[128,4,128]{2,1,0:T(4,128)} %get-tuple-element.70.refs_0_.a_own, f32[128,4,128]{2,1,0:T(4,128)} %get-tuple-element.29.a_next, ...), custom_call_target="tpu_custom_call" | custom-call | tf_op jit(solution)/shard_map/adjoint/pallas_call | solution.py:528
  (7 shorter events, 0.1 us)
Async XLA Ops:
  3.5 7.4 %copy-start = (f32[128,3,128]{2,0,1:T(8,128)S(1)}, f32[128,3,128]{2,0,1:T(8,128)}, u32[]{:S(2)}) copy-start(f32[128,3,128]{2,0,1:T(8,128)} %param.9) | copy-start | bytes 589828
  9.4 1.6 copy-start.1
  10.8 0.8 copy-start.2
  10.8 0.8 copy-start.3
